TPU v7x, 128 devices: a whole 4x4x4 slice. The times are simulated.
128 devices in a mesh: grp: 4 (over z), ep: 32 (over x, y, core).
Axes of the slice: x: 4, y: 4, z: 4, core: 2. Of those that a mesh axis runs over, the one named last changes fastest.
Arguments:
- tokens: bfloat16 [4, 2048, 3584], P('grp', 'ep'), may hold values from -6 to 6
- route_ids: int32 [4, 2048, 8], P('grp', 'ep'), may hold values from 0 to 63, as said below
- route_gates: bfloat16 [4, 2048, 8], P('grp', 'ep'), may hold values from 0.049804688 to 0.59765625
- w_gate: bfloat16 [4, 32, 3584, 1024], P('grp', 'ep'), may hold values from -0.09375 to 0.09375
- w_up: bfloat16 [4, 32, 3584, 1024], P('grp', 'ep'), may hold values from -0.09375 to 0.09375
- w_down: bfloat16 [4, 32, 1024, 3584], P('grp', 'ep'), may hold values from -0.1875 to 0.1875
- hot_source: int32 [32], P('ep'), may hold values from 0 to 3
Outputs:
- moe_output: bfloat16 [4, 2048, 3584], P('grp', 'ep')
Inputs may be any that keep to these rules, and one draw needn't show every extreme that they name: `route_ids`: each row names 8 different slots of its group. No slot is named by more than 16 rows of one device, and in each group some slot is named by exactly 16 rows of every device.
All inputs are finite; a program needn't handle non-finite values.
Results may differ from a plain program's by a relative error of at most 0.0057.
Values may be sent and summed in bfloat16 or wider, within the bound.
No kernel may reach another device: no remote copies, remote signals or barrier semaphores. Data moves between devices by JAX's collectives and lax.ppermute only.
A program may use at most 192 MiB of HBM per device.

v0:
```python
import jax
import jax.numpy as jnp
from jax import lax
from jax.sharding import PartitionSpec as P


def broadcast(shard, axis, root):
    mine = lax.axis_index(axis) == root
    return lax.psum(jnp.where(mine, shard, jnp.zeros_like(shard)), axis)


def expert_apply(inputs, weight_gate, weight_up, weight_down):
    gate_part = jnp.dot(inputs, weight_gate, preferred_element_type=jnp.float32)
    up_part = jnp.dot(inputs, weight_up, preferred_element_type=jnp.float32)
    hidden = (jax.nn.silu(gate_part) * up_part).astype(jnp.bfloat16)
    return jnp.dot(hidden, weight_down, preferred_element_type=jnp.float32).astype(jnp.bfloat16)


def arrival_places(slot_ids, slot_count):
    onehot = (slot_ids[..., None] == jnp.arange(slot_count, dtype=jnp.int32)).astype(jnp.int32)
    before = jnp.cumsum(onehot, axis=-2) - onehot
    return jnp.sum(before * onehot, axis=-1)


def local(tokens, route_ids, route_gates, w_gate, w_up, w_down, hot_source):
    devices = lax.axis_size("ep")
    beam_rows = tokens[0]
    slot_ids = route_ids[0]
    gate_vals = route_gates[0]
    row_count = beam_rows.shape[0]
    feature_count = beam_rows.shape[1]
    pick_count = slot_ids.shape[1]
    capacity = row_count * pick_count // devices
    owner_rows = devices * capacity
    own_gate = w_gate[0, 0]
    own_up = w_up[0, 0]
    own_down = w_down[0, 0]
    donor_group = hot_source[0]
    flat_ids = slot_ids.reshape(-1)
    target = flat_ids * capacity + arrival_places(flat_ids, 2 * devices)
    senders = jnp.arange(row_count * pick_count, dtype=jnp.int32) // pick_count
    lookup_table = jnp.full((2 * owner_rows,), row_count, jnp.int32).at[target].set(senders)
    padded = jnp.concatenate([beam_rows, jnp.zeros((1, feature_count), beam_rows.dtype)], axis=0)
    outgoing = padded[lookup_table].reshape(2, devices, capacity, feature_count)
    arrived_rows = lax.all_to_all(outgoing, "ep", split_axis=1, concat_axis=1, tiled=True)
    slot_rows = arrived_rows.reshape(2, owner_rows, feature_count)
    own_out = expert_apply(slot_rows[0], own_gate, own_up, own_down)
    hot_gate, hot_up, hot_down = (
        broadcast(own_gate, "grp", donor_group),
        broadcast(own_up, "grp", donor_group),
        broadcast(own_down, "grp", donor_group),
    )
    hot_out = expert_apply(slot_rows[1], hot_gate, hot_up, hot_down)
    outbox = jnp.stack([own_out, hot_out])
    returned_rows = lax.all_to_all(
        outbox.reshape(2, devices, capacity, feature_count),
        "ep",
        split_axis=1,
        concat_axis=1,
        tiled=True,
    )
    results = returned_rows.reshape(2 * owner_rows, feature_count)[target].reshape(
        row_count, pick_count, feature_count
    )
    combined = jnp.einsum("rkd,rk->rd", results, gate_vals, preferred_element_type=jnp.float32)
    return combined.astype(jnp.bfloat16)[None]


def solution(mesh):
    placed = (
        P("grp", "ep", None),
        P("grp", "ep", None),
        P("grp", "ep", None),
        P("grp", "ep", None, None),
        P("grp", "ep", None, None),
        P("grp", "ep", None, None),
        P("ep"),
    )
    return jax.shard_map(
        local, mesh=mesh, in_specs=placed, out_specs=P("grp", "ep", None), check_vma=False
    )
```

profile of v0, /device:TPU:0, one launch (start us, length us, event | category | flops | bytes accessed | tf_op | source)
XLA Modules:
  0.0 575.7 jit_solution(3451460797912001406)
XLA Ops:
  7.2 6.7 %bitcast_select_fusion = bf16[1024,3584]{1,0:T(8,128)(2,1)} fusion(bf16[1,1,1024,3584]{3,2,1,0:T(8,128)(2,1)} %param.12, pred[]{:T(512)S(6)} %eq.38), kind=kLoop, calls=%fused_computation.4 | loop fusion | flops 3670016 | bytes 14680065 | tf_op jit(solution)/shard_map/jit(_where)/select_n | solution.py:9
  13.9 8.7 %bitcast_select_fusion.1 = (bf16[3584,1024]{1,0:T(8,128)(2,1)}, bf16[3584,1024]{1,0:T(8,128)(2,1)}) fusion(bf16[1,1,3584,1024]{3,2,1,0:T(8,128)(2,1)S(1)} %copy-done, pred[]{:T(512)S(6)} %eq.38, bf16[1,1,3584,1024]{3,2,1,0:T(8,128)(2,1)} %param.10), kind=kLoop, calls=%fused_computation.7 | loop fusion | flops 7340032 | bytes 29360128 | tf_op jit(solution)/shard_map/jit(_where)/select_n | solution.py:9
  22.6 0.0 all-reduce.4.cloned.1.call-update
  22.6 0.7 copy-done.2
  23.2 0.1 copy.13
  23.3 0.1 eq.30
  23.4 0.1 eq.34
  23.5 0.1 copy.12
  23.6 0.1 mul.34
  23.7 1.2 reduce-window.6
  24.9 0.2 slice_reduce_fusion
  25.3 0.1 fusion.18
  25.4 2.4 scatter_custom_fusion
  27.9 7.3 %gather_fusion = bf16[1024,3584]{1,0:T(8,128)(2,1)} fusion(bf16[65,3584]{1,0:T(8,128)(2,1)S(1)} %concatenate.4, s32[1024]{0:T(1024)S(1)} %fusion.20), kind=kCustom, calls=%fused_computation | custom fusion | bytes 14684160 | tf_op jit(solution)/shard_map/gather | solution.py:44
  35.1 3.8 copy.16
  38.9 0.0 slice-start
  38.9 91.7 %all_to_all.10 = bf16[2,32,16,3584]{3,2,0,1:T(8,128)(2,1)S(1)} all-to-all(bf16[2,32,16,3584]{3,2,0,1:T(8,128)(2,1)S(1)} %copy.16), channel_id=1, replica_groups=mesh['grp'=4,'ep'=32] {'ep'}, dimensions={1} | all-to-all | bytes 14680064 | tf_op jit(solution)/shard_map/all_to_all | solution.py:45
  130.6 3.9 fusion.28
  134.4 0.1 slice-done.1
  134.5 7.3 %fusion.2 = f32[512,1024]{1,0:T(8,128)} fusion(bf16[512,3584]{1,0:T(8,128)(2,1)} %bitcast.81, bf16[1,1,3584,1024]{3,2,1,0:T(8,128)(2,1)S(1)} %bitcast.76), kind=kOutput, calls=%fused_computation.8 | convolution fusion | flops 3758096384 | bytes 13107200 | tf_op jit(solution)/shard_map/dot_general | solution.py:14
  141.8 17.3 %fusion.6 = bf16[512,3584]{1,0:T(8,128)(2,1)} fusion(bf16[1,1,1024,3584]{3,2,1,0:T(8,128)(2,1)} %param.12, f32[512,1024]{1,0:T(8,128)} %fusion.2, bf16[512,3584]{1,0:T(8,128)(2,1)} %bitcast.82, bf16[1,1,3584,1024]{3,2,1,0:T(8,128)(2,1)} %param.10), kind=kOutput, calls=%fused_computation.13 | convolution fusion | flops 7521173504 | bytes 24117248 | tf_op jit(solution)/shard_map/dot_general | solution.py:16
  159.1 247.4 %all-reduce.4.cloned.1.call-done = (bf16[1024,3584]{1,0:T(8,128)(2,1)}, bf16[3584,1024]{1,0:T(8,128)(2,1)}, bf16[3584,1024]{1,0:T(8,128)(2,1)}) async-done(((bf16[1024,3584]{1,0:T(8,128)(2,1)}, bf16[3584,1024]{1,0:T(8,128)(2,1)}, bf16[3584,1024]{1,0:T(8,128)(2,1)}), (bf16[1024,3584]{1,0:T(8,128)(2,1)}, bf16[3584,1024]{1,0:T(8,128)(2,1)}, bf16[3584,1024]{1,0:T(8,128)(2,1)})) %all-reduce.4.cloned.1.call-update) | async-done | bytes 22020112 | tf_op jit(solution)/shard_map/psum | solution.py:9
  406.4 9.5 %fusion.29 = f32[512,1024]{1,0:T(8,128)} fusion(bf16[512,3584]{1,0:T(8,128)(2,1)} %bitcast.77, bf16[3584,1024]{1,0:T(8,128)(2,1)} %get-tuple-element.6), kind=kOutput, calls=%fused_computation.47 | convolution fusion | flops 3758096384 | bytes 13107200 | tf_op jit(solution)/shard_map/dot_general | solution.py:13
  416.0 16.6 %convolution_convert_fusion = bf16[512,3584]{1,0:T(8,128)(2,1)} fusion(bf16[1024,3584]{1,0:T(8,128)(2,1)} %get-tuple-element.5, f32[512,1024]{1,0:T(8,128)} %fusion.29, bf16[512,3584]{1,0:T(8,128)(2,1)} %bitcast.78, bf16[3584,1024]{1,0:T(8,128)(2,1)} %get-tuple-element.7), kind=kOutput, calls=%fused_computation.14 | convolution fusion | flops 7521173504 | bytes 24117248 | tf_op jit(solution)/shard_map/dot_general | solution.py:16
  432.6 6.8 %pad_maximum_fusion = bf16[2,32,16,3584]{3,2,0,1:T(8,128)(2,1)} fusion(bf16[1,32,16,3584]{3,2,0,1:T(8,128)(2,1)} %bitcast.80, bf16[1,32,16,3584]{3,2,0,1:T(8,128)(2,1)} %bitcast.79), kind=kLoop, calls=%fused_computation.3 | loop fusion | flops 3670016 | bytes 14680064 | tf_op jit(solution)/shard_map/stack | solution.py:54
  439.4 7.3 %all-to-all-start.1 = ((bf16[2,32,16,3584]{3,2,0,1:T(8,128)(2,1)}), bf16[2,32,16,3584]{3,2,0,1:T(8,128)(2,1)}, u32[]{:S(2)}, u32[]{:S(2)}) async-start(bf16[2,32,16,3584]{3,2,0,1:T(8,128)(2,1)} %pad_maximum_fusion), calls=%async_computation.1 | async-start | bytes 14680064 | tf_op jit(solution)/shard_map/all_to_all | solution.py:55
  446.7 0.1 copy.20
  446.8 99.5 %all-to-all-done.1 = bf16[2,32,16,3584]{3,2,0,1:T(8,128)(2,1)} async-done(((bf16[2,32,16,3584]{3,2,0,1:T(8,128)(2,1)}), bf16[2,32,16,3584]{3,2,0,1:T(8,128)(2,1)}, u32[]{:S(2)}, u32[]{:S(2)}) %all-to-all-start.1) | async-done | bytes 7340064 | tf_op jit(solution)/shard_map/all_to_all | solution.py:55
  546.4 6.6 %copy.19 = bf16[2,32,16,3584]{3,2,1,0:T(8,128)(2,1)} copy(bf16[2,32,16,3584]{3,2,0,1:T(8,128)(2,1)} %all-to-all-done.1) | data formatting | bytes 14680064 | tf_op jit(solution)/shard_map/all_to_all | solution.py:55
  553.0 11.9 %gather_fusion.1 = bf16[512,3584]{1,0:T(8,128)(2,1)} fusion(bf16[1024,3584]{1,0:T(8,128)(2,1)} %bitcast.73, s32[1024]{0:T(1024)S(1)} %pad_clamp_fusion), kind=kCustom, calls=%fused_computation.1 | custom fusion | bytes 7342080 | tf_op jit(solution)/shard_map/gather | solution.py:62
  564.9 3.1 fusion.9
  568.1 0.8 copy.27
  (20 shorter events, 0.1 us)
Async XLA Ops:
  6.5 399.9 %all-reduce.4.cloned.1.call-start = ((), (), s32[]{:S(2)}) async-start(), calls=%async_computation.2 | async-start | bytes 44040192 | tf_op jit(solution)/shard_map/psum | solution.py:9
  7.2 6.7 %copy-start = (bf16[1,1,3584,1024]{3,2,1,0:T(8,128)(2,1)S(1)}, bf16[1,1,3584,1024]{3,2,1,0:T(8,128)(2,1)}, u32[]{:S(2)}) copy-start(bf16[1,1,3584,1024]{3,2,1,0:T(8,128)(2,1)} %param.11) | copy-start | bytes 22020100
  22.6 0.7 copy-start.2
  22.6 2.6 copy-start.1
  38.9 95.5 %slice-start = ((s8[7340032]{0:T(1024)(128)(4,1)}), s8[3145728]{0:T(1024)(128)(4,1)S(1)}, s32[]{:S(2)}) async-start(s8[7340032]{0:T(1024)(128)(4,1)} %bitcast.75), calls=%async_computation.3 | async-start | bytes 6291456
  130.6 3.9 slice-start.1
  439.4 7.4 %copy-start.3 = (bf16[1,64,8]{1,2,0:T(8,128)(2,1)S(1)}, bf16[1,64,8]{1,2,0:T(8,128)(2,1)}, u32[]{:S(2)}) copy-start(bf16[1,64,8]{1,2,0:T(8,128)(2,1)} %param.9) | copy-start | bytes 3076
  439.4 107.0 %all-to-all-start.1 = ((bf16[2,32,16,3584]{3,2,0,1:T(8,128)(2,1)}), bf16[2,32,16,3584]{3,2,0,1:T(8,128)(2,1)}, u32[]{:S(2)}, u32[]{:S(2)}) async-start(bf16[2,32,16,3584]{3,2,0,1:T(8,128)(2,1)} %pad_maximum_fusion), calls=%async_computation.1 | async-start | bytes 14680064 | tf_op jit(solution)/shard_map/all_to_all | solution.py:55
Sparse Core Ops, SparseCore 0:
  22.7 383.6 all-reduce.3
where the time goes:
time: 586 us; the launch traced here: 576 us
  waiting for transfers between devices  347 us (59%)
  blocking collectives  91.7 us (16%)
  matrix products  53.8 us (9%)
  local copies, waits for them, and re-layouts  38.3 us (7%)
  other arithmetic  23.5 us (4%)
  between operations  14.2 us (2%)
  starting transfers between devices  7.34 us (1%)
    psum x1, waiting for transfers between devices, broadcast(): return lax.psum(jnp.where(mine, shard, jnp.zeros_like(shard)), axis)  247 us
    all_to_all x1, waiting for transfers between devices, local(): lax.all_to_all(outbox.reshape(2, devices, capacity, feature_count), 'ep',...  99.5 us
    all_to_all x1, blocking collectives, local(): lax.all_to_all(outgoing, 'ep', split_axis=1, concat_axis=1, tiled=True)  91.7 us
    dot_general x2, matrix products, expert_apply(): jnp.dot(hidden, weight_down, preferred_element_type=jnp.float32)  33.9 us
    select_n x2, other arithmetic, broadcast(): return lax.psum(jnp.where(mine, shard, jnp.zeros_like(shard)), axis)  15.4 us
    gather x1, local copies, waits for them, and re-layouts, local(): returned_rows.reshape(2 * owner_rows, feature_count)[target]  11.9 us
  transfers between devices with their start and end apart: 2, of which 2 were waited for; matrix products, arithmetic and copies ran while one was open for 8% of the time, Pallas kernels for 0%

commit v1 on v0

v1 whole, which is shorter than its diff:
```python
import jax
import jax.numpy as jnp
from jax import lax
from jax.sharding import PartitionSpec as P

BOTH = ("grp", "ep")


def down_copy(w_down, donor, pieces):
    n = lax.axis_size("grp")
    me = lax.axis_index("grp")
    half = w_down.shape[0] // 2
    size = half // pieces
    parts = []
    for sign in (1, -1):
        mine = w_down[:half] if sign == 1 else w_down[half:]
        mine = mine.reshape(pieces, size, mine.shape[1])
        distance = lax.rem((me - donor) * sign + 2 * n, n)
        pairs = [(i, (i + sign) % n) for i in range(n)]
        held = mine
        for step in range(pieces + n - 2):
            out_index = jnp.clip(step - distance, 0, pieces - 1)
            piece = lax.dynamic_index_in_dim(held, out_index, 0, keepdims=False)
            arrived = lax.ppermute(piece, "grp", pairs)
            in_index = step - distance + 1
            place = jnp.clip(in_index, 0, pieces - 1)
            keep = (distance > 0) & (in_index >= 0) & (in_index < pieces)
            old = lax.dynamic_index_in_dim(held, place, 0, keepdims=False)
            held = lax.dynamic_update_index_in_dim(held, jnp.where(keep, arrived, old), place, 0)
        parts.append(held.reshape(half, -1))
    return jnp.concatenate(parts, axis=0)


def places(member):
    count = jnp.cumsum(member.astype(jnp.int32), axis=-1)
    return jnp.where(member, count - 1, -1)


def local(tokens, route_ids, route_gates, w_gate, w_up, w_down, hot_source):
    n_grp, n_ep = lax.axis_size("grp"), lax.axis_size("ep")
    grp, ep = lax.axis_index("grp"), lax.axis_index("ep")
    rows = tokens[0]
    row_count, width = rows.shape
    picks = route_ids.shape[2]
    capacity = row_count * picks // n_ep * n_ep
    group_rows = row_count * n_ep
    donor = hot_source[0]
    own_gate, own_up, own_down = w_gate[0, 0], w_up[0, 0], w_down[0, 0]

    info = jnp.concatenate([route_ids[0].astype(jnp.bfloat16), route_gates[0]], axis=1)
    info = lax.all_gather(info.reshape(-1), BOTH, tiled=True).reshape(n_grp, group_rows, 2 * picks)
    every = lax.all_gather(rows, BOTH, tiled=True).reshape(n_grp, group_rows, width)
    hot_down = down_copy(own_down, donor, 8)

    ids = info[:, :, :picks].astype(jnp.int32)
    gates = info[:, :, picks:]
    my_ids = lax.dynamic_index_in_dim(ids, grp, 0, keepdims=False)
    my_gates = lax.dynamic_index_in_dim(gates, grp, 0, keepdims=False)
    own_pos = places(jnp.any(my_ids == ep, axis=-1))
    hot_pos = places(jnp.any(ids == ep + n_ep, axis=-1))
    my_hot_pos = lax.dynamic_index_in_dim(hot_pos, grp, 0, keepdims=False)
    own_scale = jnp.sum(jnp.where(my_ids == ep, my_gates, 0), axis=-1)
    hot_scale = jnp.sum(jnp.where(my_ids == ep + n_ep, my_gates, 0), axis=-1)

    slots = jnp.arange(capacity, dtype=jnp.int32)
    mine = lax.dynamic_index_in_dim(every, grp, 0, keepdims=False)
    own_pick = (own_pos[None, :] == slots[:, None]).astype(jnp.bfloat16)
    hot_pick = (hot_pos[:, None, :] == slots[None, :, None]).astype(jnp.bfloat16)
    own_rows = jnp.dot(own_pick, mine, preferred_element_type=jnp.float32).astype(jnp.bfloat16)
    hot_rows = jnp.einsum("gpr,grd->gpd", hot_pick, every, preferred_element_type=jnp.float32).astype(jnp.bfloat16)

    def hidden_of(inputs):
        gate_part = jnp.dot(inputs, own_gate, preferred_element_type=jnp.float32)
        up_part = jnp.dot(inputs, own_up, preferred_element_type=jnp.float32)
        return (jax.nn.silu(gate_part) * up_part).astype(jnp.bfloat16)

    own_hidden = hidden_of(own_rows)
    hot_hidden = hidden_of(hot_rows.reshape(n_grp * capacity, width))
    hot_hidden = jnp.where(donor == grp, hot_hidden, jnp.zeros_like(hot_hidden))
    hot_hidden = lax.psum_scatter(hot_hidden, "grp", tiled=True)

    own_out = jnp.dot(own_hidden, own_down, preferred_element_type=jnp.float32).astype(jnp.bfloat16)
    hot_out = jnp.dot(hot_hidden, hot_down, preferred_element_type=jnp.float32).astype(jnp.bfloat16)
    own_put = jnp.where(own_pos[:, None] == slots[None, :], own_scale[:, None], 0).astype(jnp.bfloat16)
    hot_put = jnp.where(my_hot_pos[:, None] == slots[None, :], hot_scale[:, None], 0).astype(jnp.bfloat16)
    partial = jnp.dot(own_put, own_out, preferred_element_type=jnp.float32) + jnp.dot(
        hot_put, hot_out, preferred_element_type=jnp.float32
    )
    return lax.psum_scatter(partial.astype(jnp.bfloat16), "ep", tiled=True)[None]


def solution(mesh):
    placed = (
        P("grp", "ep", None),
        P("grp", "ep", None),
        P("grp", "ep", None),
        P("grp", "ep", None, None),
        P("grp", "ep", None, None),
        P("grp", "ep", None, None),
        P("ep"),
    )
    return jax.shard_map(
        local, mesh=mesh, in_specs=placed, out_specs=P("grp", "ep", None), check_vma=False
    )
```

time: 586 us -> 550 us (0.939)
  waiting for transfers between devices: 347 us -> 245 us
  matrix products: 53.8 us -> 155 us
  blocking collectives: 91.7 us -> 47.7 us
  starting transfers between devices: 7.34 us -> 30.6 us
  local copies, waits for them, and re-layouts: 38.3 us -> 29.9 us
    psum x1 -> x0, waiting for transfers between devices: 247 us -> none  [broadcast(): return lax.psum(jnp.where(mine, shard, jnp.zeros_like(shard)), axis)]
    ppermute x0 -> x20, waiting for transfers between devices: none -> 128 us  [down_copy(): arrived = lax.ppermute(piece, 'grp', pairs)]
    reduce_scatter x0 -> x2, waiting for transfers between devices: none -> 116 us  [the longest x1 116 us: local(): lax.psum_scatter(partial.astype(jnp.bfloat16), 'ep', tiled=True)[None]]
    dot_general x5 -> x9, matrix products: 53.8 us -> 155 us  [the longest x1 38 us: local(): jnp.einsum('gpr,grd->gpd', hot_pick, every, preferred_element_type=jnp.fl...]
    all_to_all x1 -> x0, waiting for transfers between devices: 99.5 us -> none  [local(): lax.all_to_all(outbox.reshape(2, devices, capacity, feature_count), 'ep',...]
    all_to_all x1 -> x0, blocking collectives: 91.7 us -> none  [local(): lax.all_to_all(outgoing, 'ep', split_axis=1, concat_axis=1, tiled=True)]
    all_gather x0 -> x1, blocking collectives: none -> 47.7 us  [local(): lax.all_gather(info.reshape(-1), BOTH, tiled=True)]
    ppermute x0 -> x20, starting transfers between devices: none -> 30.5 us  [down_copy(): arrived = lax.ppermute(piece, 'grp', pairs)]
  transfers between devices with their start and end apart: 2 -> 23, of which waited for: 2 -> 18; matrix products, arithmetic and copies ran while one was open for 8% -> 32% of each run, Pallas kernels for 0% -> 0%
where the time goes in v1:
time: 550 us; the launch traced here: 542 us
  waiting for transfers between devices  245 us (45%)
  matrix products  155 us (28%)
  blocking collectives  47.7 us (9%)
  starting transfers between devices  30.6 us (6%)
  local copies, waits for them, and re-layouts  29.9 us (5%)
  other arithmetic  19.4 us (4%)
  between operations  14.5 us (3%)
    ppermute x20, waiting for transfers between devices, down_copy(): arrived = lax.ppermute(piece, 'grp', pairs)  128 us
    reduce_scatter x1, waiting for transfers between devices, local(): lax.psum_scatter(partial.astype(jnp.bfloat16), 'ep', tiled=True)[None]  116 us
    all_gather x1, blocking collectives, local(): lax.all_gather(info.reshape(-1), BOTH, tiled=True)  47.7 us
    dot_general x1, matrix products, local(): jnp.einsum('gpr,grd->gpd', hot_pick, every, preferred_element_type=jnp.fl...  38 us
    ppermute x20, starting transfers between devices, down_copy(): arrived = lax.ppermute(piece, 'grp', pairs)  30.5 us
    dot_general x2, matrix products, hidden_of(): up_part = jnp.dot(inputs, own_up, preferred_element_type=jnp.float32)  25.5 us
    dot_general x1, matrix products, hidden_of(): gate_part = jnp.dot(inputs, own_gate, preferred_element_type=jnp.float32)  21 us
    dot_general x1, matrix products, local(): jnp.dot(hot_put, hot_out, preferred_element_type=jnp.float32)  19.4 us
  transfers between devices with their start and end apart: 23, of which 18 were waited for; matrix products, arithmetic and copies ran while one was open for 32% of the time, Pallas kernels for 0%

profile of v1, /device:TPU:0, one launch (start us, length us, event | category | flops | bytes accessed | tf_op | source)
XLA Modules:
  0.0 541.6 jit_solution(9599567726740153266)
XLA Ops:
  8.0 5.5 %fusion.55 = (bf16[1,1,512,3584]{3,2,1,0:T(8,128)(2,1)}, bf16[1,1,512,3584]{3,2,1,0:T(8,128)(2,1)S(1)}) fusion(bf16[1,1,1024,3584]{3,2,1,0:T(8,128)(2,1)} %param.12), kind=kLoop, calls=%fused_computation.143 | loop fusion | bytes 14680064 | tf_op jit(solution)/shard_map/slice | solution.py:16
  16.0 4.1 collective-permute-start.10
  22.4 47.7 %all_gather.6 = bf16[131072]{0:T(1024)(128)(2,1)S(1)} all-gather(bf16[1024]{0:T(1024)(128)(2,1)S(1)} %reshape.110), channel_id=1, replica_groups=mesh['grp'=4,'ep'=32] {'grp','ep'}, dimensions={0}, use_global_device_ids=true | all-gather | bytes 264192 | tf_op jit(solution)/shard_map/all_gather | solution.py:51
  86.2 18.3 %collective-permute-done.11 = bf16[64,3584]{1,0:T(8,128)(2,1)S(1)} collective-permute-done((bf16[64,3584]{1,0:T(8,128)(2,1)S(1)}, bf16[64,3584]{1,0:T(8,128)(2,1)S(1)}, u32[]{:S(2)}, u32[]{:S(2)}) %collective-permute-start.11) | collective-permute-done | bytes 458784 | tf_op jit(solution)/shard_map/ppermute | solution.py:24
  106.5 3.6 collective-permute-done.1
  112.3 15.2 %collective-permute-done.12 = bf16[64,3584]{1,0:T(8,128)(2,1)S(1)} collective-permute-done((bf16[64,3584]{1,0:T(8,128)(2,1)S(1)}, bf16[64,3584]{1,0:T(8,128)(2,1)S(1)}, u32[]{:S(2)}, u32[]{:S(2)}) %collective-permute-start.12) | collective-permute-done | bytes 458784 | tf_op jit(solution)/shard_map/ppermute | solution.py:24
  127.7 3.4 collective-permute-start.13
  131.1 4.9 collective-permute-done.2
  138.2 13.3 %collective-permute-done.13 = bf16[64,3584]{1,0:T(8,128)(2,1)S(1)} collective-permute-done((bf16[64,3584]{1,0:T(8,128)(2,1)S(1)}, bf16[64,3584]{1,0:T(8,128)(2,1)S(1)}, u32[]{:S(2)}, u32[]{:S(2)}) %collective-permute-start.13) | collective-permute-done | bytes 458784 | tf_op jit(solution)/shard_map/ppermute | solution.py:24
  151.8 3.8 collective-permute-start.14
  155.5 6.2 %collective-permute-done.3 = bf16[64,3584]{1,0:T(8,128)(2,1)S(1)} collective-permute-done((bf16[64,3584]{1,0:T(8,128)(2,1)S(1)}, bf16[64,3584]{1,0:T(8,128)(2,1)S(1)}, u32[]{:S(2)}, u32[]{:S(2)}) %collective-permute-start.3) | collective-permute-done | bytes 458784 | tf_op jit(solution)/shard_map/ppermute | solution.py:24
  164.0 11.7 %collective-permute-done.14 = bf16[64,3584]{1,0:T(8,128)(2,1)S(1)} collective-permute-done((bf16[64,3584]{1,0:T(8,128)(2,1)S(1)}, bf16[64,3584]{1,0:T(8,128)(2,1)S(1)}, u32[]{:S(2)}, u32[]{:S(2)}) %collective-permute-start.14) | collective-permute-done | bytes 458784 | tf_op jit(solution)/shard_map/ppermute | solution.py:24
  175.9 4.1 collective-permute-start.15
  179.9 7.3 %collective-permute-done.4 = bf16[64,3584]{1,0:T(8,128)(2,1)S(1)} collective-permute-done((bf16[64,3584]{1,0:T(8,128)(2,1)S(1)}, bf16[64,3584]{1,0:T(8,128)(2,1)S(1)}, u32[]{:S(2)}, u32[]{:S(2)}) %collective-permute-start.4) | collective-permute-done | bytes 458784 | tf_op jit(solution)/shard_map/ppermute | solution.py:24
  189.4 10.5 %collective-permute-done.15 = bf16[64,3584]{1,0:T(8,128)(2,1)S(1)} collective-permute-done((bf16[64,3584]{1,0:T(8,128)(2,1)S(1)}, bf16[64,3584]{1,0:T(8,128)(2,1)S(1)}, u32[]{:S(2)}, u32[]{:S(2)}) %collective-permute-start.15) | collective-permute-done | bytes 458784 | tf_op jit(solution)/shard_map/ppermute | solution.py:24
  200.1 3.8 collective-permute-start.16
  203.8 6.7 %collective-permute-done.5 = bf16[64,3584]{1,0:T(8,128)(2,1)S(1)} collective-permute-done((bf16[64,3584]{1,0:T(8,128)(2,1)S(1)}, bf16[64,3584]{1,0:T(8,128)(2,1)S(1)}, u32[]{:S(2)}, u32[]{:S(2)}) %collective-permute-start.5) | collective-permute-done | bytes 458784 | tf_op jit(solution)/shard_map/ppermute | solution.py:24
  212.7 6.3 %collective-permute-done.16 = bf16[64,3584]{1,0:T(8,128)(2,1)S(1)} collective-permute-done((bf16[64,3584]{1,0:T(8,128)(2,1)S(1)}, bf16[64,3584]{1,0:T(8,128)(2,1)S(1)}, u32[]{:S(2)}, u32[]{:S(2)}) %collective-permute-start.16) | collective-permute-done | bytes 458784 | tf_op jit(solution)/shard_map/ppermute | solution.py:24
  220.7 3.5 collective-permute-done.6
  226.4 4.4 collective-permute-done.17
  244.0 4.1 collective-permute-start.19
  249.7 38.0 %fusion.4 = bf16[4,512,3584]{2,1,0:T(8,128)(2,1)} fusion(bf16[4,2048,3584]{2,1,0:T(8,128)(2,1)} %bitcast.231, s32[4,2048]{1,0:T(4,128)S(1)} %bitcast_select_fusion.20), kind=kOutput, calls=%fused_computation.6 | convolution fusion | flops 30076305408 | bytes 73433088 | tf_op jit(solution)/shard_map/gpr,grd->gpd/dot_general | solution.py:70
  287.7 21.5 %fusion.12 = f32[2048,1024]{1,0:T(8,128)} fusion(bf16[2048,3584]{1,0:T(8,128)(2,1)} %bitcast.235, bf16[1,1,3584,1024]{3,2,1,0:T(8,128)(2,1)} %param.11), kind=kOutput, calls=%fused_computation.15 | convolution fusion | flops 15032385536 | bytes 30408704 | tf_op jit(solution)/shard_map/dot_general | solution.py:74
  309.2 21.0 %broadcast_select_fusion = bf16[2048,1024]{1,0:T(8,128)(2,1)} fusion(pred[]{:T(512)S(6)} %eq.95, f32[2048,1024]{1,0:T(8,128)} %fusion.12, bf16[2048,3584]{1,0:T(8,128)(2,1)S(1)} %bitcast.236, bf16[1,1,3584,1024]{3,2,1,0:T(8,128)(2,1)} %param.10), kind=kOutput, calls=%fused_computation.31 | convolution fusion | flops 15047065600 | bytes 34603008 | tf_op jit(solution)/shard_map/dot_general | solution.py:73
  332.5 9.0 %collective-permute-done.9 = bf16[64,3584]{1,0:T(8,128)(2,1)S(1)} collective-permute-done((bf16[64,3584]{1,0:T(8,128)(2,1)S(1)}, bf16[64,3584]{1,0:T(8,128)(2,1)S(1)}, u32[]{:S(2)}, u32[]{:S(2)}) %collective-permute-start.9) | collective-permute-done | bytes 458784 | tf_op jit(solution)/shard_map/ppermute | solution.py:24
  342.4 11.4 %fusion.23 = bf16[512,3584]{1,0:T(8,128)(2,1)S(1)} fusion(bf16[4,2048,3584]{2,1,0:T(8,128)(2,1)} %bitcast.232, s32[]{:T(128)S(6)} %select_n.238, s32[2048]{0:T(1024)S(1)} %copy-done.3), kind=kOutput, calls=%fused_computation.24 | convolution fusion | flops 7519076352 | bytes 18358276 | tf_op jit(solution)/shard_map/dot_general | solution.py:69
  355.7 3.9 fusion.14
  359.6 16.1 %fusion.20 = bf16[512,3584]{1,0:T(8,128)(2,1)} fusion(bf16[1,1,1024,3584]{3,2,1,0:T(8,128)(2,1)} %param.12, f32[512,1024]{1,0:T(8,128)S(1)} %fusion.14, bf16[512,3584]{1,0:T(8,128)(2,1)} %copy-done.10, bf16[1,1,3584,1024]{3,2,1,0:T(8,128)(2,1)} %param.10), kind=kOutput, calls=%fused_computation.23 | convolution fusion | flops 7521173504 | bytes 24117248 | tf_op jit(solution)/shard_map/dot_general | solution.py:82
  375.8 15.8 %fusion.36 = f32[2048,3584]{1,0:T(8,128)} fusion(bf16[512,3584]{1,0:T(8,128)(2,1)} %fusion.20, s32[2048]{0:T(1024)S(1)} %copy-done.3, bf16[2048]{0:T(1024)(128)(2,1)S(1)} %copy-done.6), kind=kOutput, calls=%fused_computation.33 | convolution fusion | flops 7518289920 | bytes 33042432 | tf_op jit(solution)/shard_map/dot_general | solution.py:86
  391.6 7.4 %fusion.26 = bf16[512,3584]{1,0:T(8,128)(2,1)S(1)} fusion(bf16[512,1024]{1,0:T(8,128)(2,1)} %reduce-scatter.3.cloned.1.call-done, bf16[512,3584]{1,0:T(8,128)(2,1)} %bitcast.226, bf16[512,3584]{1,0:T(8,128)(2,1)} %bitcast.43), kind=kOutput, calls=%fused_computation.25 | convolution fusion | flops 3774611456 | bytes 12058624 | tf_op jit(solution)/shard_map/dot_general | solution.py:83
  399.1 19.4 %add_convert_fusion = bf16[2048,3584]{1,0:T(8,128)(2,1)} fusion(f32[2048,3584]{1,0:T(8,128)} %fusion.36, bf16[512,3584]{1,0:T(8,128)(2,1)S(1)} %fusion.26, s32[2048]{0:T(1024)S(1)} %bitcast.229, bf16[2048]{0:T(1024)(128)(2,1)S(1)} %copy-done.5), kind=kOutput, calls=%fused_computation | convolution fusion | flops 7532969984 | bytes 47722496 | tf_op jit(solution)/shard_map/dot_general | solution.py:86
  418.5 116.3 %reduce-scatter.5.cloned.1.call-done = bf16[64,3584]{1,0:T(8,128)(2,1)} async-done(((bf16[2048,3584]{1,0:T(8,128)(2,1)}), bf16[64,3584]{1,0:T(8,128)(2,1)}) %reduce-scatter.5.cloned.1.call-update) | async-done | bytes 458768 | tf_op jit(solution)/shard_map/reduce_scatter | solution.py:89
  (118 shorter events, 58.7 us)
Async XLA Ops:
  6.5 243.2 %all-gather.3.cloned.1.call-start = ((), (), s32[]{:S(2)}) async-start(), calls=%async_computation.4 | async-start | bytes 59179008 | tf_op jit(solution)/shard_map/all_gather | solution.py:52
  7.3 384.3 %reduce-scatter.3.cloned.1.call-start = ((), (), s32[]{:S(2)}) async-start(), calls=%async_computation.2 | async-start | bytes 5242880 | tf_op jit(solution)/shard_map/reduce_scatter | solution.py:80
  13.4 8.8 %copy-start.7 = (s32[1,64,8]{1,2,0:T(8,128)S(1)}, s32[1,64,8]{1,2,0:T(8,128)}, u32[]{:S(2)}) copy-start(s32[1,64,8]{1,2,0:T(8,128)} %param.8) | copy-start | bytes 6148
  13.4 8.8 %copy-start.8 = (bf16[1,64,8]{1,2,0:T(8,128)(2,1)S(1)}, bf16[1,64,8]{1,2,0:T(8,128)(2,1)}, u32[]{:S(2)}) copy-start(bf16[1,64,8]{1,2,0:T(8,128)(2,1)} %param.9) | copy-start | bytes 3076
  16.0 62.9 %collective-permute-start.10 = (bf16[64,3584]{1,0:T(8,128)(2,1)}, bf16[64,3584]{1,0:T(8,128)(2,1)}, u32[]{:S(2)}, u32[]{:S(2)}) collective-permute-start(bf16[64,3584]{1,0:T(8,128)(2,1)} %get-tuple-element.49), channel_id=1, source_target_pairs={{0,96},{32,0},{64,32},{96,64},{1,97},{33,1},{65,33},{97,65},{2,98}... | collective-permute-start | bytes 1376264 | tf_op jit(solution)/shard_map/ppermute | solution.py:24
  22.2 59.9 %collective-permute-start = (bf16[64,3584]{1,0:T(8,128)(2,1)}, bf16[64,3584]{1,0:T(8,128)(2,1)}, u32[]{:S(2)}, u32[]{:S(2)}) collective-permute-start(bf16[64,3584]{1,0:T(8,128)(2,1)} %get-tuple-element.29), channel_id=1, source_target_pairs={{0,32},{32,64},{64,96},{96,0},{1,33},{33,65},{65,97},{97,1},{2,34}... | collective-permute-start | bytes 1376264 | tf_op jit(solution)/shard_map/ppermute | solution.py:24
  79.8 24.7 %copy-start.1 = (bf16[8,64,3584]{2,1,0:T(8,128)(2,1)S(1)}, bf16[8,64,3584]{2,1,0:T(8,128)(2,1)}, u32[]{:S(2)}) copy-start(bf16[8,64,3584]{2,1,0:T(8,128)(2,1)} %bitcast_dynamic-update-slice_fusion.9) | copy-start | bytes 11010052
  81.5 23.0 %collective-permute-start.11 = (bf16[64,3584]{1,0:T(8,128)(2,1)S(1)}, bf16[64,3584]{1,0:T(8,128)(2,1)S(1)}, u32[]{:S(2)}, u32[]{:S(2)}) collective-permute-start(bf16[64,3584]{1,0:T(8,128)(2,1)S(1)} %get-tuple-element.47), channel_id=1, source_target_pairs={{0,96},{32,0},{64,32},{96,64},{1,97},{33,1},{65,33},{97,65},{2,98}... | collective-permute-start | bytes 1376264 | tf_op jit(solution)/shard_map/ppermute | solution.py:24
  86.1 24.0 %collective-permute-start.1 = (bf16[64,3584]{1,0:T(8,128)(2,1)S(1)}, bf16[64,3584]{1,0:T(8,128)(2,1)S(1)}, u32[]{:S(2)}, u32[]{:S(2)}) collective-permute-start(bf16[64,3584]{1,0:T(8,128)(2,1)S(1)} %get-tuple-element.27), channel_id=1, source_target_pairs={{0,32},{32,64},{64,96},{96,0},{1,33},{33,65},{65,97},{97,1},{2,34}... | collective-permute-start | bytes 1376264 | tf_op jit(solution)/shard_map/ppermute | solution.py:24
  104.7 22.8 %collective-permute-start.12 = (bf16[64,3584]{1,0:T(8,128)(2,1)S(1)}, bf16[64,3584]{1,0:T(8,128)(2,1)S(1)}, u32[]{:S(2)}, u32[]{:S(2)}) collective-permute-start(bf16[64,3584]{1,0:T(8,128)(2,1)S(1)} %get-tuple-element.45), channel_id=1, source_target_pairs={{0,96},{32,0},{64,32},{96,64},{1,97},{33,1},{65,33},{97,65},{2,98}... | collective-permute-start | bytes 1376264 | tf_op jit(solution)/shard_map/ppermute | solution.py:24
  112.3 23.8 %collective-permute-start.2 = (bf16[64,3584]{1,0:T(8,128)(2,1)S(1)}, bf16[64,3584]{1,0:T(8,128)(2,1)S(1)}, u32[]{:S(2)}, u32[]{:S(2)}) collective-permute-start(bf16[64,3584]{1,0:T(8,128)(2,1)S(1)} %get-tuple-element.25), channel_id=1, source_target_pairs={{0,32},{32,64},{64,96},{96,0},{1,33},{33,65},{65,97},{97,1},{2,34}... | collective-permute-start | bytes 1376264 | tf_op jit(solution)/shard_map/ppermute | solution.py:24
  127.7 23.9 %collective-permute-start.13 = (bf16[64,3584]{1,0:T(8,128)(2,1)S(1)}, bf16[64,3584]{1,0:T(8,128)(2,1)S(1)}, u32[]{:S(2)}, u32[]{:S(2)}) collective-permute-start(bf16[64,3584]{1,0:T(8,128)(2,1)S(1)} %get-tuple-element.43), channel_id=1, source_target_pairs={{0,96},{32,0},{64,32},{96,64},{1,97},{33,1},{65,33},{97,65},{2,98}... | collective-permute-start | bytes 1376264 | tf_op jit(solution)/shard_map/ppermute | solution.py:24
  138.2 23.6 %collective-permute-start.3 = (bf16[64,3584]{1,0:T(8,128)(2,1)S(1)}, bf16[64,3584]{1,0:T(8,128)(2,1)S(1)}, u32[]{:S(2)}, u32[]{:S(2)}) collective-permute-start(bf16[64,3584]{1,0:T(8,128)(2,1)S(1)} %get-tuple-element.23), channel_id=1, source_target_pairs={{0,32},{32,64},{64,96},{96,0},{1,33},{33,65},{65,97},{97,1},{2,34}... | collective-permute-start | bytes 1376264 | tf_op jit(solution)/shard_map/ppermute | solution.py:24
  151.8 23.9 %collective-permute-start.14 = (bf16[64,3584]{1,0:T(8,128)(2,1)S(1)}, bf16[64,3584]{1,0:T(8,128)(2,1)S(1)}, u32[]{:S(2)}, u32[]{:S(2)}) collective-permute-start(bf16[64,3584]{1,0:T(8,128)(2,1)S(1)} %get-tuple-element.41), channel_id=1, source_target_pairs={{0,96},{32,0},{64,32},{96,64},{1,97},{33,1},{65,33},{97,65},{2,98}... | collective-permute-start | bytes 1376264 | tf_op jit(solution)/shard_map/ppermute | solution.py:24
  163.9 23.3 %collective-permute-start.4 = (bf16[64,3584]{1,0:T(8,128)(2,1)S(1)}, bf16[64,3584]{1,0:T(8,128)(2,1)S(1)}, u32[]{:S(2)}, u32[]{:S(2)}) collective-permute-start(bf16[64,3584]{1,0:T(8,128)(2,1)S(1)} %get-tuple-element.21), channel_id=1, source_target_pairs={{0,32},{32,64},{64,96},{96,0},{1,33},{33,65},{65,97},{97,1},{2,34}... | collective-permute-start | bytes 1376264 | tf_op jit(solution)/shard_map/ppermute | solution.py:24
  175.9 24.0 %collective-permute-start.15 = (bf16[64,3584]{1,0:T(8,128)(2,1)S(1)}, bf16[64,3584]{1,0:T(8,128)(2,1)S(1)}, u32[]{:S(2)}, u32[]{:S(2)}) collective-permute-start(bf16[64,3584]{1,0:T(8,128)(2,1)S(1)} %get-tuple-element.39), channel_id=1, source_target_pairs={{0,96},{32,0},{64,32},{96,64},{1,97},{33,1},{65,33},{97,65},{2,98}... | collective-permute-start | bytes 1376264 | tf_op jit(solution)/shard_map/ppermute | solution.py:24
  189.3 21.2 %collective-permute-start.5 = (bf16[64,3584]{1,0:T(8,128)(2,1)S(1)}, bf16[64,3584]{1,0:T(8,128)(2,1)S(1)}, u32[]{:S(2)}, u32[]{:S(2)}) collective-permute-start(bf16[64,3584]{1,0:T(8,128)(2,1)S(1)} %get-tuple-element.19), channel_id=1, source_target_pairs={{0,32},{32,64},{64,96},{96,0},{1,33},{33,65},{65,97},{97,1},{2,34}... | collective-permute-start | bytes 1376264 | tf_op jit(solution)/shard_map/ppermute | solution.py:24
  200.1 18.9 %collective-permute-start.16 = (bf16[64,3584]{1,0:T(8,128)(2,1)S(1)}, bf16[64,3584]{1,0:T(8,128)(2,1)S(1)}, u32[]{:S(2)}, u32[]{:S(2)}) collective-permute-start(bf16[64,3584]{1,0:T(8,128)(2,1)S(1)} %get-tuple-element.37), channel_id=1, source_target_pairs={{0,96},{32,0},{64,32},{96,64},{1,97},{33,1},{65,33},{97,65},{2,98}... | collective-permute-start | bytes 1376264 | tf_op jit(solution)/shard_map/ppermute | solution.py:24
  212.6 11.6 %collective-permute-start.6 = (bf16[64,3584]{1,0:T(8,128)(2,1)S(1)}, bf16[64,3584]{1,0:T(8,128)(2,1)S(1)}, u32[]{:S(2)}, u32[]{:S(2)}) collective-permute-start(bf16[64,3584]{1,0:T(8,128)(2,1)S(1)} %get-tuple-element.17), channel_id=1, source_target_pairs={{0,32},{32,64},{64,96},{96,0},{1,33},{33,65},{65,97},{97,1},{2,34}... | collective-permute-start | bytes 1376264 | tf_op jit(solution)/shard_map/ppermute | solution.py:24
  219.1 11.7 %collective-permute-start.17 = (bf16[64,3584]{1,0:T(8,128)(2,1)S(1)}, bf16[64,3584]{1,0:T(8,128)(2,1)S(1)}, u32[]{:S(2)}, u32[]{:S(2)}) collective-permute-start(bf16[64,3584]{1,0:T(8,128)(2,1)S(1)} %get-tuple-element.35), channel_id=1, source_target_pairs={{0,96},{32,0},{64,32},{96,64},{1,97},{33,1},{65,33},{97,65},{2,98}... | collective-permute-start | bytes 1376264 | tf_op jit(solution)/shard_map/ppermute | solution.py:24
  226.3 10.6 %collective-permute-start.7 = (bf16[64,3584]{1,0:T(8,128)(2,1)S(1)}, bf16[64,3584]{1,0:T(8,128)(2,1)S(1)}, u32[]{:S(2)}, u32[]{:S(2)}) collective-permute-start(bf16[64,3584]{1,0:T(8,128)(2,1)S(1)} %get-tuple-element.15), channel_id=1, source_target_pairs={{0,32},{32,64},{64,96},{96,0},{1,33},{33,65},{65,97},{97,1},{2,34}... | collective-permute-start | bytes 1376264 | tf_op jit(solution)/shard_map/ppermute | solution.py:24
  231.0 10.9 %collective-permute-start.18 = (bf16[64,3584]{1,0:T(8,128)(2,1)S(1)}, bf16[64,3584]{1,0:T(8,128)(2,1)S(1)}, u32[]{:S(2)}, u32[]{:S(2)}) collective-permute-start(bf16[64,3584]{1,0:T(8,128)(2,1)S(1)} %get-tuple-element.33), channel_id=1, source_target_pairs={{0,96},{32,0},{64,32},{96,64},{1,97},{33,1},{65,33},{97,65},{2,98}... | collective-permute-start | bytes 1376264 | tf_op jit(solution)/shard_map/ppermute | solution.py:24
  239.1 9.8 %collective-permute-start.8 = (bf16[64,3584]{1,0:T(8,128)(2,1)S(1)}, bf16[64,3584]{1,0:T(8,128)(2,1)S(1)}, u32[]{:S(2)}, u32[]{:S(2)}) collective-permute-start(bf16[64,3584]{1,0:T(8,128)(2,1)S(1)} %get-tuple-element.13), channel_id=1, source_target_pairs={{0,32},{32,64},{64,96},{96,0},{1,33},{33,65},{65,97},{97,1},{2,34}... | collective-permute-start | bytes 1376264 | tf_op jit(solution)/shard_map/ppermute | solution.py:24
  244.0 87.6 %collective-permute-start.19 = (bf16[64,3584]{1,0:T(8,128)(2,1)S(1)}, bf16[64,3584]{1,0:T(8,128)(2,1)S(1)}, u32[]{:S(2)}, u32[]{:S(2)}) collective-permute-start(bf16[64,3584]{1,0:T(8,128)(2,1)S(1)} %get-tuple-element.31), channel_id=1, source_target_pairs={{0,96},{32,0},{64,32},{96,64},{1,97},{33,1},{65,33},{97,65},{2,98}... | collective-permute-start | bytes 1376264 | tf_op jit(solution)/shard_map/ppermute | solution.py:24
  287.7 21.5 %copy-start.9 = (bf16[4,512,3584]{2,1,0:T(8,128)(2,1)S(1)}, bf16[4,512,3584]{2,1,0:T(8,128)(2,1)}, u32[]{:S(2)}) copy-start(bf16[4,512,3584]{2,1,0:T(8,128)(2,1)} %fusion.4) | copy-start | bytes 44040196
  330.2 12.2 %copy-start.3 = (s32[2048]{0:T(1024)S(1)}, s32[2048]{0:T(1024)}, u32[]{:S(2)}) copy-start(s32[2048]{0:T(1024)} %bitcast_select_fusion.21) | copy-start | bytes 24580
  330.2 204.6 %reduce-scatter.5.cloned.1.call-start = ((), (), s32[]{:S(2)}) async-start(), calls=%async_computation.3 | async-start | bytes 15138816 | tf_op jit(solution)/shard_map/reduce_scatter | solution.py:89
  331.5 10.0 %collective-permute-start.9 = (bf16[64,3584]{1,0:T(8,128)(2,1)S(1)}, bf16[64,3584]{1,0:T(8,128)(2,1)S(1)}, u32[]{:S(2)}, u32[]{:S(2)}) collective-permute-start(bf16[64,3584]{1,0:T(8,128)(2,1)S(1)} %get-tuple-element.11), channel_id=1, source_target_pairs={{0,32},{32,64},{64,96},{96,0},{1,33},{33,65},{65,97},{97,1},{2,34}... | collective-permute-start | bytes 1376264 | tf_op jit(solution)/shard_map/ppermute | solution.py:24
  331.6 24.1 %slice-start = ((s8[7340032]{0:T(1024)(128)(4,1)}), s8[4194304]{0:T(1024)(128)(4,1)S(1)}, s32[]{:S(2)}) async-start(s8[7340032]{0:T(1024)(128)(4,1)} %bitcast.233), calls=%async_computation.5 | async-start | bytes 8388608
  342.4 13.3 %slice-start.1 = ((s8[7340032]{0:T(1024)(128)(4,1)}), s8[3145728]{0:T(1024)(128)(4,1)S(1)}, s32[]{:S(2)}) async-start(s8[7340032]{0:T(1024)(128)(4,1)} %bitcast.233), calls=%async_computation.6 | async-start | bytes 6291456
  359.6 16.1 %copy-start.6 = (bf16[2048]{0:T(1024)(128)(2,1)S(1)}, bf16[2048]{0:T(1024)(128)(2,1)}, u32[]{:S(2)}) copy-start(bf16[2048]{0:T(1024)(128)(2,1)} %get-tuple-element.6) | copy-start | bytes 12292
  391.6 7.5 %copy-start.5 = (bf16[2048]{0:T(1024)(128)(2,1)S(1)}, bf16[2048]{0:T(1024)(128)(2,1)}, u32[]{:S(2)}) copy-start(bf16[2048]{0:T(1024)(128)(2,1)} %get-tuple-element.5) | copy-start | bytes 12292
  (4 other events, 12.9 us)
Sparse Core Ops, SparseCore 0:
  10.3 210.1 all-gather.2
  330.4 47.2 reduce-scatter.2
  418.6 116.1 reduce-scatter.4

commit v2 on v1

v2 whole, which is shorter than its diff:
```python
import functools

import jax
import jax.numpy as jnp
from jax import lax
from jax.experimental import pallas as pl
from jax.experimental.pallas import tpu as pltpu
from jax.sharding import PartitionSpec as P

SIDE = 4
BLOCK = 4
WINDOW = 128
ALIGN = 64
TILE = 128
EARLY = (0, 1, 3)
LATE = (2,)
VMEM = 58 * 1024 * 1024


def ep_of(x, y, core):
    return (x * SIDE + y) * 2 + core


def moved(index, ring, step):
    x, y, core = index // (2 * SIDE), index // 2 % SIDE, index % 2
    if (ring == 0) == (core == 0):
        return ep_of(x, (y + step) % SIDE, core)
    return ep_of((x + step) % SIDE, y, core)


def shift_z(value, step):
    return lax.ppermute(value, "grp", [(i, (i + step) % SIDE) for i in range(SIDE)])


def shift_ring(value, ring, step):
    count = 2 * SIDE * SIDE
    return lax.ppermute(value, "ep", [(i, moved(i, ring, step)) for i in range(count)])


def swap_cores(value):
    count = 2 * SIDE * SIDE
    return lax.ppermute(value, "ep", [(i, i ^ 1) for i in range(count)])


def down_copy(w_down, distance, pieces):
    half = w_down.shape[0] // 2
    size = half // pieces
    parts = []
    for sign in (1, -1):
        held = w_down[:half] if sign == 1 else w_down[half:]
        held = held.reshape(pieces, size, held.shape[1])
        away = distance if sign == 1 else lax.rem(SIDE - distance, SIDE)
        for step in range(pieces + SIDE - 2):
            piece = lax.dynamic_index_in_dim(held, jnp.clip(step - away, 0, pieces - 1), 0, keepdims=False)
            arrived = shift_z(piece, sign)
            index = step - away + 1
            place = jnp.clip(index, 0, pieces - 1)
            keep = (away > 0) & (index >= 0) & (index < pieces)
            old = lax.dynamic_index_in_dim(held, place, 0, keepdims=False)
            held = lax.dynamic_update_index_in_dim(held, jnp.where(keep, arrived, old), place, 0)
        parts.append(held.reshape(half, -1))
    return parts


def hidden_kernel(blocks, capacity, sources, meta, places, gate_hbm, up_hbm, *rest):
    count = max(piece for block in sources for piece, _ in block) + 1
    pieces = rest[:count]
    own_out, hot_out, gate, up, gathered, compact, weight_sems, row_sems = rest[count:]
    rows = pieces[0].shape[2]
    width = gate.shape[0]
    hidden = gate.shape[1]
    block_rows = BLOCK * rows
    wide = 512 if width % 512 == 0 else 256
    me = meta[0]
    donates = meta[1] == 1

    def load(distance, slot):
        for block, units in enumerate(sources):
            for unit, (piece, place) in enumerate(units):
                pltpu.make_async_copy(
                    pieces[piece].at[place, distance],
                    gathered.at[slot, pl.ds(block * block_rows + unit * rows, rows)],
                    row_sems.at[slot],
                ).start()

    def arrive(slot):
        pltpu.make_async_copy(gathered.at[slot], gathered.at[slot], row_sems.at[slot]).wait()

    def serve(segment, slot, store):
        compact[...] = jnp.zeros_like(compact)

        def pick(block, carry):
            start = meta[2 + segment * (blocks + 1) + block]
            start = pl.multiple_of(start, ALIGN)
            place = places[pl.ds(segment * blocks + block, 1), :] - start
            slots = lax.broadcasted_iota(jnp.int32, (WINDOW, block_rows), 0)
            choose = jnp.where(slots == place, 1.0, 0.0).astype(jnp.bfloat16)

            def part(n, carry):
                columns = pl.ds(pl.multiple_of(n * wide, wide), wide)
                values = gathered[slot, pl.ds(pl.multiple_of(block * block_rows, block_rows), block_rows), columns]
                found = jnp.dot(choose, values, preferred_element_type=jnp.float32).astype(jnp.bfloat16)
                compact[pl.ds(start, WINDOW), columns] = compact[pl.ds(start, WINDOW), columns] + found
                return carry

            return lax.fori_loop(0, width // wide, part, carry)

        lax.fori_loop(0, blocks, pick, 0)

        def tile(t, carry):
            span = pl.ds(pl.multiple_of(t * TILE, TILE), TILE)

            def part(n, carry):
                columns = pl.ds(pl.multiple_of(n * 256, 256), 256)
                gate_part = jnp.dot(compact[span, :], gate[:, columns], preferred_element_type=jnp.float32)
                up_part = jnp.dot(compact[span, :], up[:, columns], preferred_element_type=jnp.float32)
                store(span, columns, (jax.nn.silu(gate_part) * up_part).astype(jnp.bfloat16))
                return carry

            return lax.fori_loop(0, hidden // 256, part, carry)

        lax.fori_loop(0, meta[2 + segment * (blocks + 1) + blocks], tile, 0)

    weights = (
        pltpu.make_async_copy(gate_hbm, gate, weight_sems.at[0]),
        pltpu.make_async_copy(up_hbm, up, weight_sems.at[1]),
    )
    load(0, 0)
    for copy in weights:
        copy.start()
    own_out[...] = jnp.zeros_like(own_out)
    hot_out[...] = jnp.zeros_like(hot_out)

    def own_store(span, columns, value):
        own_out[span, columns] = value

    for distance in range(SIDE):
        slot = distance % 2
        group = lax.rem(me + distance, SIDE)

        def hot_store(span, columns, value, group=group):
            hot_out[group, span, columns] = value

        if distance < SIDE - 1:
            pl.when(donates)(functools.partial(load, distance + 1, 1 - slot))
        if distance == 0:
            arrive(slot)
            for copy in weights:
                copy.wait()
            serve(0, slot, own_store)
        else:
            pl.when(donates)(functools.partial(arrive, slot))
        pl.when(donates)(functools.partial(serve, 1 + distance, slot, hot_store))


def hidden_call(blocks, capacity, sources, meta, places, gate, up, pieces):
    rows = pieces[0].shape[2]
    width, hidden = gate.shape
    block_rows = BLOCK * rows
    anywhere = pl.BlockSpec(memory_space=pl.ANY)
    tiles = 5 * capacity // TILE
    return pl.pallas_call(
        functools.partial(hidden_kernel, blocks, capacity, sources),
        in_specs=[pl.BlockSpec(memory_space=pltpu.SMEM), pl.BlockSpec(memory_space=pltpu.VMEM)]
        + [anywhere] * (2 + len(pieces)),
        out_specs=[pl.BlockSpec(memory_space=pltpu.VMEM)] * 2,
        out_shape=[
            jax.ShapeDtypeStruct((capacity, hidden), jnp.bfloat16),
            jax.ShapeDtypeStruct((SIDE, capacity, hidden), jnp.bfloat16),
        ],
        scratch_shapes=[
            pltpu.VMEM((width, hidden), jnp.bfloat16),
            pltpu.VMEM((width, hidden), jnp.bfloat16),
            pltpu.VMEM((2, blocks * block_rows, width), jnp.bfloat16),
            pltpu.VMEM((capacity, width), jnp.bfloat16),
            pltpu.SemaphoreType.DMA((2,)),
            pltpu.SemaphoreType.DMA((2,)),
        ],
        compiler_params=pltpu.CompilerParams(vmem_limit_bytes=VMEM),
        cost_estimate=pl.CostEstimate(
            flops=tiles * TILE * width * hidden * 4,
            bytes_accessed=2 * width * hidden * 2 + 4 * blocks * block_rows * width * 2,
            transcendentals=tiles * TILE * hidden,
        ),
    )(meta, places, gate, up, *pieces)


def combine_kernel(starts, routes, own_early, own_late, hot_early, hot_late, down, copied_low, copied_high,
                   mine, theirs, outs, pair):
    early = own_early.shape[0]
    late = own_late.shape[0]
    half = copied_low.shape[0]
    total = early + late
    block_rows = mine.shape[0] // SIDE

    def put(begin, size, value):
        outs[pl.ds(begin, size), :] = value.astype(jnp.bfloat16)

    put(0, early, jnp.dot(own_early[...], down[...], preferred_element_type=jnp.float32))
    put(early, late, jnp.dot(own_late[...], down[...], preferred_element_type=jnp.float32))
    for begin, size, ref in ((total, early, hot_early), (total + early, late, hot_late)):
        put(
            begin,
            size,
            jnp.dot(ref[:, :half], copied_low[...], preferred_element_type=jnp.float32)
            + jnp.dot(ref[:, half:], copied_high[...], preferred_element_type=jnp.float32),
        )

    for out, first in ((theirs, SIDE), (mine, 0)):

        def block(b, carry, out=out, first=first):
            own_start = pl.multiple_of(starts[2 * (first + b)], ALIGN)
            hot_start = pl.multiple_of(starts[2 * (first + b) + 1], ALIGN)
            span = pl.ds(pl.multiple_of((first + b) * block_rows, block_rows), block_rows)
            slots = lax.broadcasted_iota(jnp.int32, (block_rows, WINDOW), 1).astype(jnp.float32)
            own = jnp.where(routes[span, 0:1] - own_start.astype(jnp.float32) == slots, routes[span, 1:2], 0.0)
            hot = jnp.where(routes[span, 2:3] - hot_start.astype(jnp.float32) == slots, routes[span, 3:4], 0.0)
            scale = jnp.concatenate([own.astype(jnp.bfloat16), hot.astype(jnp.bfloat16)], axis=1)
            pair[:WINDOW, :] = outs[pl.ds(own_start, WINDOW), :]
            pair[WINDOW:, :] = outs[pl.ds(total + hot_start, WINDOW), :]
            value = jnp.dot(scale, pair[...], preferred_element_type=jnp.float32)
            out[pl.ds(pl.multiple_of(b * block_rows, block_rows), block_rows), :] = value.astype(jnp.bfloat16)
            return carry

        lax.fori_loop(0, SIDE, block, 0)


def combine_call(part, parts, starts, routes, own_early, own_late, hot_early, hot_late, down, copied_low, copied_high):
    width = down.shape[1] // parts
    wide = 256
    steps = width // wide
    rows = routes.shape[0]
    whole = pl.BlockSpec(memory_space=pltpu.VMEM)
    offset = part * steps
    column = lambda ref: pl.BlockSpec((ref.shape[0], wide), lambda n: (0, offset + n))
    result = pl.BlockSpec((rows // 2, wide), lambda n: (0, n))
    slots = 2 * (own_early.shape[0] + own_late.shape[0])
    hidden = down.shape[0]
    return pl.pallas_call(
        combine_kernel,
        grid=(steps,),
        in_specs=[pl.BlockSpec(memory_space=pltpu.SMEM)] + [whole] * 5 + [column(down), column(copied_low), column(copied_high)],
        out_specs=[result, result],
        out_shape=[jax.ShapeDtypeStruct((rows // 2, width), jnp.bfloat16)] * 2,
        scratch_shapes=[pltpu.VMEM((slots, wide), jnp.bfloat16), pltpu.VMEM((2 * WINDOW, wide), jnp.bfloat16)],
        compiler_params=pltpu.CompilerParams(vmem_limit_bytes=VMEM),
        cost_estimate=pl.CostEstimate(
            flops=2 * slots * hidden * width + 4 * rows * WINDOW * width,
            bytes_accessed=4 * hidden * width + 2 * rows * width,
            transcendentals=0,
        ),
    )(starts, routes, own_early, own_late, hot_early, hot_late, down, copied_low, copied_high)


def add(*values):
    return sum(v.astype(jnp.float32) for v in values).astype(jnp.bfloat16)


def sum_to_owners(mine, theirs, rows):
    width = mine.shape[1]
    theirs = swap_cores(theirs)
    total = add(mine, theirs).reshape(SIDE, SIDE, rows, width)
    for ring, shape in ((1, (SIDE, rows, width)), (0, (rows, width))):
        cut = shape[0] // 2
        ahead = shift_ring(total[2, :cut], ring, 1)
        behind = shift_ring(total[2, cut:], ring, -1)
        forward = jnp.concatenate([add(total[1, :cut], ahead), total[1, cut:]], axis=0)
        backward = jnp.concatenate([total[3, :cut], add(total[3, cut:], behind)], axis=0)
        total = add(total[0], shift_ring(forward, ring, 1), shift_ring(backward, ring, -1))
    return total


def local(tokens, route_ids, route_gates, w_gate, w_up, w_down, hot_source):
    n_ep = lax.axis_size("ep")
    grp, ep = lax.axis_index("grp"), lax.axis_index("ep")
    rows = tokens[0]
    row_count, width = rows.shape
    picks = route_ids.shape[2]
    cap = row_count * picks // n_ep
    donor = hot_source[0]
    own_gate, own_up, own_down = w_gate[0, 0], w_up[0, 0], w_down[0, 0]

    info = jnp.concatenate([route_ids[0].astype(jnp.bfloat16), route_gates[0]], axis=1)
    info = lax.all_gather(info.reshape(-1), ("grp", "ep"), tiled=True)
    info = info.reshape(SIDE, n_ep, row_count, 2 * picks)

    below, above = shift_z(rows, 1), shift_z(rows, -1)
    cut = row_count // 2
    far = (shift_z(below[:cut], 1), shift_z(above[cut:], -1))
    unit = jnp.stack([rows, above, jnp.concatenate(far, axis=0), below])
    below, above = shift_ring(unit, 0, 1), shift_ring(unit, 0, -1)
    far = (shift_ring(below[:2], 0, 1), shift_ring(above[2:], 0, -1))
    near = jnp.stack([unit, above, jnp.concatenate(far, axis=0), below])
    below, above = shift_ring(near, 1, 1), shift_ring(near, 1, -1)
    far_low, far_high = shift_ring(below[:2], 1, 1), shift_ring(above[2:], 1, -1)
    early = [near, above, below]
    early = early + [swap_cores(piece) for piece in early]
    late = [far_low, far_high]
    late = late + [swap_cores(piece) for piece in late]

    copied_low, copied_high = down_copy(own_down, lax.rem(grp - donor + SIDE, SIDE), 8)

    core = lax.rem(ep, 2)
    x, y = ep // (2 * SIDE), lax.rem(ep // 2, SIDE)

    def source(other, second, first):
        at = jnp.where(other == 1, 1 - core, core)
        dx = jnp.where(at == 0, second, first)
        dy = jnp.where(at == 0, first, second)
        return ep_of(lax.rem(x + dx, SIDE), lax.rem(y + dy, SIDE), at)

    order = [(other, second) for seconds in (EARLY, LATE) for other in (0, 1) for second in seconds]
    units = jnp.stack([source(other, second, first) for other, second in order for first in range(SIDE)])
    groups = lax.rem(grp + jnp.arange(SIDE, dtype=jnp.int32), SIDE)
    ids = info[:, :, :, :picks].astype(jnp.int32)
    scales = info[:, :, :, picks:].astype(jnp.float32)
    is_own = (ids == ep)[grp]
    is_hot = ids == ep + n_ep
    member = jnp.concatenate([jnp.any(is_own, axis=-1)[None], jnp.any(is_hot, axis=-1)[groups]], axis=0)[:, units]
    own_scale = jnp.sum(jnp.where(is_own, scales[grp], 0.0), axis=-1)[units]
    hot_scale = jnp.sum(jnp.where(is_hot[grp], scales[grp], 0.0), axis=-1)[units]
    block_rows = BLOCK * row_count
    member = member.reshape(1 + SIDE, len(order), block_rows).astype(jnp.int32)
    donates = (donor == grp).astype(jnp.int32)

    first_late = 2 * len(EARLY)
    places, windows, metas = [], [], []
    for begin, end in ((0, first_late), (first_late, len(order))):
        blocks = end - begin
        capacity = blocks * BLOCK * cap
        here = member[:, begin:end].reshape(1 + SIDE, blocks * block_rows)
        after = jnp.cumsum(here, axis=1)
        place = jnp.where(here == 1, after - 1, -1).reshape(1 + SIDE, blocks, block_rows)
        after = after.reshape(1 + SIDE, blocks, block_rows)
        before = jnp.concatenate([jnp.zeros((1 + SIDE, 1), jnp.int32), after[:, :-1, -1]], axis=1)
        window = jnp.minimum(before // ALIGN * ALIGN, capacity - WINDOW)
        tiles = (after[:, -1, -1] + TILE - 1) // TILE
        meta = jnp.concatenate([window, tiles[:, None]], axis=1).reshape(-1)
        metas.append(jnp.concatenate([jnp.stack([grp, donates]), meta]))
        places.append(place)
        windows.append(window)

    pieces_of = {0: lambda o: o * 3, 1: lambda o: o * 3 + 1, 3: lambda o: o * 3 + 2}
    early_sources = [[(pieces_of[second](other), first) for first in range(SIDE)] for other, second in order[:first_late]]
    late_sources = [[(other * 2 + first // 2, first % 2) for first in range(SIDE)] for other, _ in order[first_late:]]
    own_hidden, hot_hidden = [], []
    for sources, pieces, place, meta in (
        (early_sources, early, places[0], metas[0]),
        (late_sources, late, places[1], metas[1]),
    ):
        blocks = len(sources)
        own, hot = hidden_call(
            blocks, blocks * BLOCK * cap, sources, meta, place.reshape(-1, block_rows), own_gate, own_up, pieces
        )
        own_hidden.append(own)
        hot_hidden.append(lax.psum_scatter(hot.reshape(-1, hot.shape[2]), "grp", tiled=True))

    early_slots = first_late * BLOCK * cap
    place = jnp.concatenate([places[0][:2], jnp.where(places[1][:2] < 0, -1, places[1][:2] + early_slots)], axis=1)
    window = jnp.concatenate([windows[0][:2], windows[1][:2] + early_slots], axis=1)
    wanted = [order.index((other, second)) for other in (0, 1) for second in range(SIDE)]
    scale = jnp.stack([own_scale, hot_scale]).reshape(2, len(order), block_rows)
    take = lambda value: jnp.stack([value[:, index] for index in wanted], axis=1)
    place, window, scale = take(place), take(window), take(scale)
    starts = window.T.reshape(-1)
    routes = jnp.stack([place[0].astype(jnp.float32), scale[0], place[1].astype(jnp.float32), scale[1]], axis=-1)
    routes = routes.reshape(len(order) * block_rows, 4)

    parts = 2
    results = []
    for part in range(parts):
        mine, theirs = combine_call(
            part, parts, starts, routes, own_hidden[0], own_hidden[1], hot_hidden[0], hot_hidden[1],
            own_down, copied_low, copied_high,
        )
        results.append(sum_to_owners(mine, theirs, row_count))
    return jnp.concatenate(results, axis=1)[None]


def solution(mesh):
    placed = (
        P("grp", "ep", None),
        P("grp", "ep", None),
        P("grp", "ep", None),
        P("grp", "ep", None, None),
        P("grp", "ep", None, None),
        P("grp", "ep", None, None),
        P("ep"),
    )
    return jax.shard_map(
        local, mesh=mesh, in_specs=placed, out_specs=P("grp", "ep", None), check_vma=False
    )
```

time: 550 us -> 595 us (1.082)
  matrix products: 155 us -> 0 us
  starting transfers between devices: 30.6 us -> 143 us
  Pallas kernels: 0 us -> 93.2 us
  waiting for transfers between devices: 245 us -> 201 us
  other arithmetic: 19.4 us -> 42.4 us
  local copies, waits for them, and re-layouts: 29.9 us -> 51.6 us
  blocking collectives: 47.7 us -> 39.6 us
    dot_general x9 -> x0, matrix products: 155 us -> none  [the longest x1 38 us: local(): jnp.einsum('gpr,grd->gpd', hot_pick, every, preferred_element_type=jnp.fl...]
    ppermute x20 -> x55, starting transfers between devices: 30.5 us -> 143 us  [the longest x24 104 us: shift_z(): lax.ppermute(value, 'grp', [(i, (i + step) % SIDE) for i in range(SIDE)])]
    reduce_scatter x2, waiting for transfers between devices: 116 us -> 7.76 us  [local(): lax.psum_scatter(hot.reshape(-1, hot.shape[2]), 'grp', tiled=True)]
    pallas_call x0 -> x4, Pallas kernels: none -> 93.2 us  [the longest x2 53.6 us: combine_call(): pl.pallas_call(combine_kernel, grid=(steps,), in_specs=[pl.BlockSpec(memo...]
    ppermute x20 -> x55, waiting for transfers between devices: 128 us -> 193 us  [the longest x24 117 us: shift_ring(): lax.ppermute(value, 'ep', [(i, moved(i, ring, step)) for i in range(count)])]
    dynamic_slice x20, local copies, waits for them, and re-layouts: 16.4 us -> 25.9 us  [down_copy(): old = lax.dynamic_index_in_dim(held, place, 0, keepdims=False)]
    convert_element_type x1 -> x12, other arithmetic: 0.01 us -> 8.47 us  [the longest x10 5.21 us: add(): return sum((v.astype(jnp.float32) for v in values)).astype(jnp.bfloat16)]
    slice x2 -> x25, local copies, waits for them, and re-layouts: 5.54 us -> 13.9 us  [the longest x1 6.63 us: down_copy(): held = w_down[:half] if sign == 1 else w_down[half:]]
  transfers between devices with their start and end apart: 23 -> 57, of which waited for: 18 -> 28; matrix products, arithmetic and copies ran while one was open for 32% -> 15% of each run, Pallas kernels for 0% -> 11%
where the time goes in v2:
time: 595 us; the launch traced here: 586 us
  waiting for transfers between devices  201 us (34%)
  starting transfers between devices  143 us (24%)
  Pallas kernels  93.2 us (16%)
  local copies, waits for them, and re-layouts  51.6 us (9%)
  other arithmetic  42.4 us (7%)
  blocking collectives  39.6 us (7%)
  between operations  15.8 us (3%)
    ppermute x24, waiting for transfers between devices, shift_ring(): lax.ppermute(value, 'ep', [(i, moved(i, ring, step)) for i in range(count)])  117 us
    ppermute x24, starting transfers between devices, shift_z(): lax.ppermute(value, 'grp', [(i, (i + step) % SIDE) for i in range(SIDE)])  104 us
    ppermute x24, waiting for transfers between devices, shift_z(): lax.ppermute(value, 'grp', [(i, (i + step) % SIDE) for i in range(SIDE)])  73.9 us
    pallas_call x2, Pallas kernels, combine_call(): pl.pallas_call(combine_kernel, grid=(steps,), in_specs=[pl.BlockSpec(memo...  53.6 us
    all_gather x1, blocking collectives, local(): info = lax.all_gather(info.reshape(-1), ('grp', 'ep'), tiled=True)  39.6 us
    pallas_call x2, Pallas kernels, hidden_call(): pl.pallas_call(functools.partial(hidden_kernel, blocks, capacity, sources...  39.6 us
    ppermute x24, starting transfers between devices, shift_ring(): lax.ppermute(value, 'ep', [(i, moved(i, ring, step)) for i in range(count)])  36.8 us
    dynamic_slice x20, local copies, waits for them, and re-layouts, down_copy(): old = lax.dynamic_index_in_dim(held, place, 0, keepdims=False)  25.9 us
  transfers between devices with their start and end apart: 57, of which 28 were waited for; matrix products, arithmetic and copies ran while one was open for 15% of the time, Pallas kernels for 11%

profile of v2, /device:TPU:0, one launch (start us, length us, event | category | flops | bytes accessed | tf_op | source)
XLA Modules:
  0.0 586.3 jit_solution(14766270033312833331)
XLA Ops:
  11.3 6.6 %fusion.40 = (bf16[1,1,512,3584]{3,2,1,0:T(8,128)(2,1)}, bf16[1,1,512,3584]{3,2,1,0:T(8,128)(2,1)}) fusion(bf16[1,1,1024,3584]{3,2,1,0:T(8,128)(2,1)} %param.12), kind=kLoop, calls=%fused_computation.241 | loop fusion | bytes 14680064 | tf_op jit(solution)/shard_map/slice | solution.py:50
  25.4 39.6 %all_gather.3 = bf16[131072]{0:T(1024)(128)(2,1)S(1)} all-gather(bf16[1024]{0:T(1024)(128)(2,1)S(1)} %reshape.1556), channel_id=1, replica_groups=mesh['grp'=4,'ep'=32] {'grp','ep'}, dimensions={0}, use_global_device_ids=true | all-gather | bytes 264192 | tf_op jit(solution)/shard_map/all_gather | solution.py:284
  90.9 3.8 collective-permute-start.28
  100.3 4.1 collective-permute-done.18
  112.0 7.4 %collective-permute-done.19 = bf16[64,3584]{1,0:T(8,128)(2,1)S(1)} collective-permute-done((bf16[64,3584]{1,0:T(8,128)(2,1)S(1)}, bf16[64,3584]{1,0:T(8,128)(2,1)S(1)}, u32[]{:S(2)}, u32[]{:S(2)}) %collective-permute-start.19) | collective-permute-done | bytes 458784 | tf_op jit(solution)/shard_map/ppermute | solution.py:32
  123.8 3.3 collective-permute-start.30
  129.4 4.2 collective-permute-done.20
  135.8 4.8 collective-permute-done.7
  152.9 4.8 collective-permute-done.31
  164.1 4.6 collective-permute-done.32
  174.2 55.7 %collective-permute-done.9.rest_2_ = bf16[4,4,64,3584]{3,2,1,0:T(8,128)(2,1)S(1)} collective-permute-done((bf16[4,4,64,3584]{3,2,1,0:T(8,128)(2,1)S(1)}, bf16[4,4,64,3584]{3,2,1,0:T(8,128)(2,1)S(1)}, u32[]{:S(2)}, u32[]{:S(2)}) %collective-permute-start.9) | collective-permute-done | bytes 7340064 | tf_op jit(solution)/shard_map/ppermute | solution.py:37
  245.7 6.6 %collective-permute-done.24 = bf16[64,3584]{1,0:T(8,128)(2,1)S(1)} collective-permute-done((bf16[64,3584]{1,0:T(8,128)(2,1)S(1)}, bf16[64,3584]{1,0:T(8,128)(2,1)S(1)}, u32[]{:S(2)}, u32[]{:S(2)}) %collective-permute-start.24) | collective-permute-done | bytes 458784 | tf_op jit(solution)/shard_map/ppermute | solution.py:32
  255.6 22.9 %collective-permute-done.13.rest_0_ = bf16[2,4,64,3584]{3,2,1,0:T(8,128)(2,1)} collective-permute-done((bf16[2,4,64,3584]{3,2,1,0:T(8,128)(2,1)}, bf16[2,4,64,3584]{3,2,1,0:T(8,128)(2,1)}, u32[]{:S(2)}, u32[]{:S(2)}) %collective-permute-start.13) | collective-permute-done | bytes 3670048 | tf_op jit(solution)/shard_map/ppermute | solution.py:37
  278.4 3.6 collective-permute-done.14.rest_1_
  290.4 13.9 %shard_map.74 = (bf16[128,1024]{1,0:T(8,128)(2,1)}, bf16[4,128,1024]{2,1,0:T(8,128)(2,1)}) custom-call(s32[17]{0:T(128)} %pad_add_fusion.4.meta, s32[10,256]{1,0:T(8,128)} %broadcast_select_fusion.1.places, bf16[3584,1024]{1,0:T(8,128)(2,1)} %bitcast.391, bf16[3584,1024]{1,0:T(8,128)(2,1)} %bitcast.393, ...), custom_call_target="tpu_custom_call" | custom-call | flops 9395240960 | bytes 29360128 | tf_op jit(solution)/shard_map/pallas_call | solution.py:162
  304.4 25.7 %shard_map.73 = (bf16[384,1024]{1,0:T(8,128)(2,1)}, bf16[4,384,1024]{2,1,0:T(8,128)(2,1)}) custom-call(s32[37]{0:T(128)} %pad_add_fusion.3.meta, s32[30,256]{1,0:T(8,128)} %broadcast_select_fusion.places, bf16[3584,1024]{1,0:T(8,128)(2,1)} %bitcast.392, bf16[3584,1024]{1,0:T(8,128)(2,1)} %bitcast.394, bf16[4,4,64,3584]{3,2,1,0:T(8,128)(2,1)} %copy-done, ...), custom_call_target="tpu_custom_call" | custom-call | flops 28185722880 | bytes 58720256 | tf_op jit(solution)/shard_map/pallas_call | solution.py:162
  333.6 3.3 collective-permute-start.35
  336.9 16.8 %collective-permute-done.25 = bf16[64,3584]{1,0:T(8,128)(2,1)S(1)} collective-permute-done((bf16[64,3584]{1,0:T(8,128)(2,1)S(1)}, bf16[64,3584]{1,0:T(8,128)(2,1)S(1)}, u32[]{:S(2)}, u32[]{:S(2)}) %collective-permute-start.25) | collective-permute-done | bytes 458784 | tf_op jit(solution)/shard_map/ppermute | solution.py:32
  355.8 72.5 %collective-permute-start.26 = (bf16[64,3584]{1,0:T(8,128)(2,1)S(1)}, bf16[64,3584]{1,0:T(8,128)(2,1)S(1)}, u32[]{:S(2)}, u32[]{:S(2)}) collective-permute-start(bf16[64,3584]{1,0:T(8,128)(2,1)S(1)} %get-tuple-element.65), channel_id=1, source_target_pairs={{0,32},{32,64},{64,96},{96,0},{1,33},{33,65},{65,97},{97,1},{2,34}... | collective-permute-start | bytes 1376264 | tf_op jit(solution)/shard_map/ppermute | solution.py:32
  433.1 13.0 %collective-permute-done.26 = bf16[64,3584]{1,0:T(8,128)(2,1)S(1)} collective-permute-done((bf16[64,3584]{1,0:T(8,128)(2,1)S(1)}, bf16[64,3584]{1,0:T(8,128)(2,1)S(1)}, u32[]{:S(2)}, u32[]{:S(2)}) %collective-permute-start.26) | collective-permute-done | bytes 458784 | tf_op jit(solution)/shard_map/ppermute | solution.py:32
  447.0 8.9 %collective-permute-done.36 = bf16[64,3584]{1,0:T(8,128)(2,1)S(1)} collective-permute-done((bf16[64,3584]{1,0:T(8,128)(2,1)S(1)}, bf16[64,3584]{1,0:T(8,128)(2,1)S(1)}, u32[]{:S(2)}, u32[]{:S(2)}) %collective-permute-start.36) | collective-permute-done | bytes 458784 | tf_op jit(solution)/shard_map/ppermute | solution.py:32
  456.8 7.8 %reduce-scatter.3.cloned.1.call-done.hot_early = bf16[384,1024]{1,0:T(8,128)(2,1)} async-done(((bf16[1536,1024]{1,0:T(8,128)(2,1)}), bf16[384,1024]{1,0:T(8,128)(2,1)}) %reduce-scatter.3.cloned.1.call-update) | async-done | bytes 786448 | tf_op jit(solution)/shard_map/reduce_scatter | solution.py:356
  464.6 26.7 %shard_map.76 = (bf16[1024,1792]{1,0:T(8,128)(2,1)}, bf16[1024,1792]{1,0:T(8,128)(2,1)}) custom-call(s32[16]{0:T(128)} %reshape.1562.starts, f32[2048,4]{1,0:T(8,128)} %copy.87.routes, bf16[384,1024]{1,0:T(8,128)(2,1)} %get-tuple-element.13.own_early, bf16[128,1024]{1,0:T(8,128)(2,1)} %get-tuple-element.14.own_late, ...), custom_call_target="tpu_custom_call" | custom-call | flops 5637144576 | bytes 14680064 | tf_op jit(solution)/shard_map/pallas_call | solution.py:239
  491.5 26.9 %shard_map.75 = (bf16[1024,1792]{1,0:T(8,128)(2,1)}, bf16[1024,1792]{1,0:T(8,128)(2,1)}) custom-call(s32[16]{0:T(128)} %reshape.1562.starts, f32[2048,4]{1,0:T(8,128)} %copy.87.routes, bf16[384,1024]{1,0:T(8,128)(2,1)} %get-tuple-element.13.own_early, bf16[128,1024]{1,0:T(8,128)(2,1)} %get-tuple-element.14.own_late, ...), custom_call_target="tpu_custom_call" | custom-call | flops 5637144576 | bytes 14680064 | tf_op jit(solution)/shard_map/pallas_call | solution.py:239
  532.1 3.3 collective-permute-start.50
  537.0 3.3 collective-permute-start.41
  540.5 5.8 collective-permute-done.50
  546.3 3.8 collective-permute-done.48
  553.8 3.5 collective-permute-done.41
  557.4 3.8 collective-permute-done.39
  567.7 3.3 collective-permute-start.45
  574.6 3.8 collective-permute-done.43
  (287 shorter events, 152.2 us)
Async XLA Ops:
  6.5 450.3 %reduce-scatter.5.cloned.1.call-start = ((), (), s32[]{:S(2)}) async-start(), calls=%async_computation.3 | async-start | bytes 1310720 | tf_op jit(solution)/shard_map/reduce_scatter | solution.py:356
  6.5 78.2 %collective-permute-start.1 = (bf16[64,3584]{1,0:T(8,128)(2,1)}, bf16[64,3584]{1,0:T(8,128)(2,1)}, u32[]{:S(2)}, u32[]{:S(2)}) collective-permute-start(bf16[64,3584]{1,0:T(8,128)(2,1)} %bitcast.374), channel_id=1, source_target_pairs={{0,32},{32,64},{64,96},{96,0},{1,33},{33,65},{65,97},{97,1},{2,34}... | collective-permute-start | bytes 1376264 | tf_op jit(solution)/shard_map/ppermute | solution.py:32
  8.5 72.8 %collective-permute-start = (bf16[64,3584]{1,0:T(8,128)(2,1)}, bf16[64,3584]{1,0:T(8,128)(2,1)}, u32[]{:S(2)}, u32[]{:S(2)}) collective-permute-start(bf16[64,3584]{1,0:T(8,128)(2,1)} %bitcast.375), channel_id=1, source_target_pairs={{0,96},{32,0},{64,32},{96,64},{1,97},{33,1},{65,33},{97,65},{2,98}... | collective-permute-start | bytes 1376264 | tf_op jit(solution)/shard_map/ppermute | solution.py:32
  20.0 65.8 %collective-permute-start.17 = (bf16[64,3584]{1,0:T(8,128)(2,1)}, bf16[64,3584]{1,0:T(8,128)(2,1)}, u32[]{:S(2)}, u32[]{:S(2)}) collective-permute-start(bf16[64,3584]{1,0:T(8,128)(2,1)} %get-tuple-element.83), channel_id=1, source_target_pairs={{0,32},{32,64},{64,96},{96,0},{1,33},{33,65},{65,97},{97,1},{2,34}... | collective-permute-start | bytes 1376264 | tf_op jit(solution)/shard_map/ppermute | solution.py:32
  22.0 66.8 %collective-permute-start.27 = (bf16[64,3584]{1,0:T(8,128)(2,1)}, bf16[64,3584]{1,0:T(8,128)(2,1)}, u32[]{:S(2)}, u32[]{:S(2)}) collective-permute-start(bf16[64,3584]{1,0:T(8,128)(2,1)} %get-tuple-element.63), channel_id=1, source_target_pairs={{0,96},{32,0},{64,32},{96,64},{1,97},{33,1},{65,33},{97,65},{2,98}... | collective-permute-start | bytes 1376264 | tf_op jit(solution)/shard_map/ppermute | solution.py:32
  87.9 16.5 %collective-permute-start.18 = (bf16[64,3584]{1,0:T(8,128)(2,1)S(1)}, bf16[64,3584]{1,0:T(8,128)(2,1)S(1)}, u32[]{:S(2)}, u32[]{:S(2)}) collective-permute-start(bf16[64,3584]{1,0:T(8,128)(2,1)S(1)} %get-tuple-element.81), channel_id=1, source_target_pairs={{0,32},{32,64},{64,96},{96,0},{1,33},{33,65},{65,97},{97,1},{2,34}... | collective-permute-start | bytes 1376264 | tf_op jit(solution)/shard_map/ppermute | solution.py:32
  90.9 15.7 %collective-permute-start.28 = (bf16[64,3584]{1,0:T(8,128)(2,1)S(1)}, bf16[64,3584]{1,0:T(8,128)(2,1)S(1)}, u32[]{:S(2)}, u32[]{:S(2)}) collective-permute-start(bf16[64,3584]{1,0:T(8,128)(2,1)S(1)} %get-tuple-element.61), channel_id=1, source_target_pairs={{0,96},{32,0},{64,32},{96,64},{1,97},{33,1},{65,33},{97,65},{2,98}... | collective-permute-start | bytes 1376264 | tf_op jit(solution)/shard_map/ppermute | solution.py:32
  97.0 31.0 %collective-permute-start.5 = (bf16[4,64,3584]{2,1,0:T(8,128)(2,1)S(1)}, bf16[4,64,3584]{2,1,0:T(8,128)(2,1)S(1)}, u32[]{:S(2)}, u32[]{:S(2)}) collective-permute-start(bf16[4,64,3584]{2,1,0:T(8,128)(2,1)S(1)} %get-tuple-element.87), channel_id=1, source_target_pairs={{0,2},{1,9},{2,4},{3,11},{4,6},{5,13},{6,0},{7,15},{8,10},{9,17},{... | collective-permute-start | bytes 5505032 | tf_op jit(solution)/shard_map/ppermute | solution.py:37
  97.2 29.9 %collective-permute-start.4 = (bf16[4,64,3584]{2,1,0:T(8,128)(2,1)S(1)}, bf16[4,64,3584]{2,1,0:T(8,128)(2,1)S(1)}, u32[]{:S(2)}, u32[]{:S(2)}) collective-permute-start(bf16[4,64,3584]{2,1,0:T(8,128)(2,1)S(1)} %get-tuple-element.87), channel_id=1, source_target_pairs={{0,6},{1,25},{2,0},{3,27},{4,2},{5,29},{6,4},{7,31},{8,14},{9,1},{... | collective-permute-start | bytes 5505032 | tf_op jit(solution)/shard_map/ppermute | solution.py:37
  123.8 22.7 %collective-permute-start.30 = (bf16[64,3584]{1,0:T(8,128)(2,1)S(1)}, bf16[64,3584]{1,0:T(8,128)(2,1)S(1)}, u32[]{:S(2)}, u32[]{:S(2)}) collective-permute-start(bf16[64,3584]{1,0:T(8,128)(2,1)S(1)} %get-tuple-element.57), channel_id=1, source_target_pairs={{0,96},{32,0},{64,32},{96,64},{1,97},{33,1},{65,33},{97,65},{2,98}... | collective-permute-start | bytes 1376264 | tf_op jit(solution)/shard_map/ppermute | solution.py:32
  128.0 14.7 %collective-permute-start.6 = (bf16[2,64,3584]{2,1,0:T(8,128)(2,1)S(1)}, bf16[2,64,3584]{2,1,0:T(8,128)(2,1)S(1)}, u32[]{:S(2)}, u32[]{:S(2)}) collective-permute-start(bf16[2,64,3584]{2,1,0:T(8,128)(2,1)S(1)} %slice.349), channel_id=1, source_target_pairs={{0,2},{1,9},{2,4},{3,11},{4,6},{5,13},{6,0},{7,15},{8,10},{9,17},{... | collective-permute-start | bytes 2752520 | tf_op jit(solution)/shard_map/ppermute | solution.py:37
  143.9 90.1 %collective-permute-start.8 = (bf16[4,4,64,3584]{3,2,1,0:T(8,128)(2,1)S(1)}, bf16[4,4,64,3584]{3,2,1,0:T(8,128)(2,1)S(1)}, u32[]{:S(2)}, u32[]{:S(2)}) collective-permute-start(bf16[4,4,64,3584]{3,2,1,0:T(8,128)(2,1)S(1)} %pad_maximum_fusion.rest_0_), channel_id=1, source_target_pairs={{0,24},{1,7},{2,26},{3,1},{4,28},{5,3},{6,30},{7,5},{8,0},{9,15},{... | collective-permute-start | bytes 22020104 | tf_op jit(solution)/shard_map/ppermute | solution.py:37
  146.5 83.4 %collective-permute-start.9 = (bf16[4,4,64,3584]{3,2,1,0:T(8,128)(2,1)S(1)}, bf16[4,4,64,3584]{3,2,1,0:T(8,128)(2,1)S(1)}, u32[]{:S(2)}, u32[]{:S(2)}) collective-permute-start(bf16[4,4,64,3584]{3,2,1,0:T(8,128)(2,1)S(1)} %pad_maximum_fusion.rest_0_), channel_id=1, source_target_pairs={{0,8},{1,3},{2,10},{3,5},{4,12},{5,7},{6,14},{7,1},{8,16},{9,11},{... | collective-permute-start | bytes 22020104 | tf_op jit(solution)/shard_map/ppermute | solution.py:37
  170.9 74.4 %collective-permute-start.33 = (bf16[64,3584]{1,0:T(8,128)(2,1)S(1)}, bf16[64,3584]{1,0:T(8,128)(2,1)S(1)}, u32[]{:S(2)}, u32[]{:S(2)}) collective-permute-start(bf16[64,3584]{1,0:T(8,128)(2,1)S(1)} %get-tuple-element.51), channel_id=1, source_target_pairs={{0,96},{32,0},{64,32},{96,64},{1,97},{33,1},{65,33},{97,65},{2,98}... | collective-permute-start | bytes 1376264 | tf_op jit(solution)/shard_map/ppermute | solution.py:32
  234.0 44.4 %collective-permute-start.13 = (bf16[2,4,64,3584]{3,2,1,0:T(8,128)(2,1)}, bf16[2,4,64,3584]{3,2,1,0:T(8,128)(2,1)}, u32[]{:S(2)}, u32[]{:S(2)}) collective-permute-start(bf16[2,4,64,3584]{3,2,1,0:T(8,128)(2,1)} %slice.352), channel_id=1, source_target_pairs={{0,8},{1,3},{2,10},{3,5},{4,12},{5,7},{6,14},{7,1},{8,16},{9,11},{... | collective-permute-start | bytes 11010056 | tf_op jit(solution)/shard_map/ppermute | solution.py:37
  238.1 44.0 %collective-permute-start.14 = (bf16[2,4,64,3584]{3,2,1,0:T(8,128)(2,1)}, bf16[2,4,64,3584]{3,2,1,0:T(8,128)(2,1)}, u32[]{:S(2)}, u32[]{:S(2)}) collective-permute-start(bf16[2,4,64,3584]{3,2,1,0:T(8,128)(2,1)} %slice.353), channel_id=1, source_target_pairs={{0,24},{1,7},{2,26},{3,1},{4,28},{5,3},{6,30},{7,5},{8,0},{9,15},{... | collective-permute-start | bytes 11010056 | tf_op jit(solution)/shard_map/ppermute | solution.py:37
  245.2 59.2 %collective-permute-start.10 = (bf16[4,4,64,3584]{3,2,1,0:T(8,128)(2,1)}, bf16[4,4,64,3584]{3,2,1,0:T(8,128)(2,1)}, u32[]{:S(2)}, u32[]{:S(2)}) collective-permute-start(bf16[4,4,64,3584]{3,2,1,0:T(8,128)(2,1)} %copy-done), channel_id=1, source_target_pairs={{0,1},{1,0},{2,3},{3,2},{4,5},{5,4},{6,7},{7,6},{8,9},{9,8},{10,11... | collective-permute-start | bytes 22020104 | tf_op jit(solution)/shard_map/ppermute | solution.py:42
  245.3 59.2 %collective-permute-start.11 = (bf16[4,4,64,3584]{3,2,1,0:T(8,128)(2,1)}, bf16[4,4,64,3584]{3,2,1,0:T(8,128)(2,1)}, u32[]{:S(2)}, u32[]{:S(2)}) collective-permute-start(bf16[4,4,64,3584]{3,2,1,0:T(8,128)(2,1)} %copy-done.3), channel_id=1, source_target_pairs={{0,1},{1,0},{2,3},{3,2},{4,5},{5,4},{6,7},{7,6},{8,9},{9,8},{10,11... | collective-permute-start | bytes 22020104 | tf_op jit(solution)/shard_map/ppermute | solution.py:42
  252.3 52.1 %collective-permute-start.12 = (bf16[4,4,64,3584]{3,2,1,0:T(8,128)(2,1)}, bf16[4,4,64,3584]{3,2,1,0:T(8,128)(2,1)}, u32[]{:S(2)}, u32[]{:S(2)}) collective-permute-start(bf16[4,4,64,3584]{3,2,1,0:T(8,128)(2,1)} %copy-done.4), channel_id=1, source_target_pairs={{0,1},{1,0},{2,3},{3,2},{4,5},{5,4},{6,7},{7,6},{8,9},{9,8},{10,11... | collective-permute-start | bytes 22020104 | tf_op jit(solution)/shard_map/ppermute | solution.py:42
  288.1 43.4 %collective-permute-start.34 = (bf16[64,3584]{1,0:T(8,128)(2,1)S(1)}, bf16[64,3584]{1,0:T(8,128)(2,1)S(1)}, u32[]{:S(2)}, u32[]{:S(2)}) collective-permute-start(bf16[64,3584]{1,0:T(8,128)(2,1)S(1)} %get-tuple-element.49), channel_id=1, source_target_pairs={{0,96},{32,0},{64,32},{96,64},{1,97},{33,1},{65,33},{97,65},{2,98}... | collective-permute-start | bytes 1376264 | tf_op jit(solution)/shard_map/ppermute | solution.py:32
  304.4 160.2 %reduce-scatter.3.cloned.1.call-start = ((), (), s32[]{:S(2)}) async-start(), calls=%async_computation.2 | async-start | bytes 3932160 | tf_op jit(solution)/shard_map/reduce_scatter | solution.py:356
  331.4 22.3 %collective-permute-start.25 = (bf16[64,3584]{1,0:T(8,128)(2,1)S(1)}, bf16[64,3584]{1,0:T(8,128)(2,1)S(1)}, u32[]{:S(2)}, u32[]{:S(2)}) collective-permute-start(bf16[64,3584]{1,0:T(8,128)(2,1)S(1)} %get-tuple-element.67), channel_id=1, source_target_pairs={{0,32},{32,64},{64,96},{96,0},{1,33},{33,65},{65,97},{97,1},{2,34}... | collective-permute-start | bytes 1376264 | tf_op jit(solution)/shard_map/ppermute | solution.py:32
  333.6 97.3 %collective-permute-start.35 = (bf16[64,3584]{1,0:T(8,128)(2,1)S(1)}, bf16[64,3584]{1,0:T(8,128)(2,1)S(1)}, u32[]{:S(2)}, u32[]{:S(2)}) collective-permute-start(bf16[64,3584]{1,0:T(8,128)(2,1)S(1)} %get-tuple-element.47), channel_id=1, source_target_pairs={{0,96},{32,0},{64,32},{96,64},{1,97},{33,1},{65,33},{97,65},{2,98}... | collective-permute-start | bytes 1376264 | tf_op jit(solution)/shard_map/ppermute | solution.py:32
  355.8 90.3 %collective-permute-start.26 = (bf16[64,3584]{1,0:T(8,128)(2,1)S(1)}, bf16[64,3584]{1,0:T(8,128)(2,1)S(1)}, u32[]{:S(2)}, u32[]{:S(2)}) collective-permute-start(bf16[64,3584]{1,0:T(8,128)(2,1)S(1)} %get-tuple-element.65), channel_id=1, source_target_pairs={{0,32},{32,64},{64,96},{96,0},{1,33},{33,65},{65,97},{97,1},{2,34}... | collective-permute-start | bytes 1376264 | tf_op jit(solution)/shard_map/ppermute | solution.py:32
  433.0 22.9 %collective-permute-start.36 = (bf16[64,3584]{1,0:T(8,128)(2,1)S(1)}, bf16[64,3584]{1,0:T(8,128)(2,1)S(1)}, u32[]{:S(2)}, u32[]{:S(2)}) collective-permute-start(bf16[64,3584]{1,0:T(8,128)(2,1)S(1)} %get-tuple-element.45), channel_id=1, source_target_pairs={{0,96},{32,0},{64,32},{96,64},{1,97},{33,1},{65,33},{97,65},{2,98}... | collective-permute-start | bytes 1376264 | tf_op jit(solution)/shard_map/ppermute | solution.py:32
  491.3 27.6 %collective-permute-start.46 = (bf16[1024,1792]{1,0:T(8,128)(2,1)}, bf16[1024,1792]{1,0:T(8,128)(2,1)}, u32[]{:S(2)}, u32[]{:S(2)}) collective-permute-start(bf16[1024,1792]{1,0:T(8,128)(2,1)} %get-tuple-element.20), channel_id=1, source_target_pairs={{0,1},{1,0},{2,3},{3,2},{4,5},{5,4},{6,7},{7,6},{8,9},{9,8},{10,11... | collective-permute-start | bytes 11010056 | tf_op jit(solution)/shard_map/ppermute | solution.py:42
  532.1 14.2 %collective-permute-start.50 = (bf16[4,64,1792]{2,1,0:T(8,128)(2,1)S(1)}, bf16[4,64,1792]{2,1,0:T(8,128)(2,1)S(1)}, u32[]{:S(2)}, u32[]{:S(2)}) collective-permute-start(bf16[4,64,1792]{2,1,0:T(8,128)(2,1)S(1)} %pad_maximum_fusion.5), channel_id=1, source_target_pairs={{0,24},{1,7},{2,26},{3,1},{4,28},{5,3},{6,30},{7,5},{8,0},{9,15},{... | collective-permute-start | bytes 2752520 | tf_op jit(solution)/shard_map/ppermute | solution.py:37
  535.5 14.7 %collective-permute-start.48 = (bf16[4,64,1792]{2,1,0:T(8,128)(2,1)S(1)}, bf16[4,64,1792]{2,1,0:T(8,128)(2,1)S(1)}, u32[]{:S(2)}, u32[]{:S(2)}) collective-permute-start(bf16[4,64,1792]{2,1,0:T(8,128)(2,1)S(1)} %pad_maximum_fusion.4), channel_id=1, source_target_pairs={{0,8},{1,3},{2,10},{3,5},{4,12},{5,7},{6,14},{7,1},{8,16},{9,11},{... | collective-permute-start | bytes 2752520 | tf_op jit(solution)/shard_map/ppermute | solution.py:37
  537.0 20.4 %collective-permute-start.41 = (bf16[4,64,1792]{2,1,0:T(8,128)(2,1)S(1)}, bf16[4,64,1792]{2,1,0:T(8,128)(2,1)S(1)}, u32[]{:S(2)}, u32[]{:S(2)}) collective-permute-start(bf16[4,64,1792]{2,1,0:T(8,128)(2,1)S(1)} %pad_maximum_fusion.3), channel_id=1, source_target_pairs={{0,24},{1,7},{2,26},{3,1},{4,28},{5,3},{6,30},{7,5},{8,0},{9,15},{... | collective-permute-start | bytes 2752520 | tf_op jit(solution)/shard_map/ppermute | solution.py:37
  540.4 20.8 %collective-permute-start.39 = (bf16[4,64,1792]{2,1,0:T(8,128)(2,1)S(1)}, bf16[4,64,1792]{2,1,0:T(8,128)(2,1)S(1)}, u32[]{:S(2)}, u32[]{:S(2)}) collective-permute-start(bf16[4,64,1792]{2,1,0:T(8,128)(2,1)S(1)} %pad_maximum_fusion.2), channel_id=1, source_target_pairs={{0,8},{1,3},{2,10},{3,5},{4,12},{5,7},{6,14},{7,1},{8,16},{9,11},{... | collective-permute-start | bytes 2752520 | tf_op jit(solution)/shard_map/ppermute | solution.py:37
  550.5 14.4 %collective-permute-start.51 = (bf16[32,1792]{1,0:T(8,128)(2,1)S(1)}, bf16[32,1792]{1,0:T(8,128)(2,1)S(1)}, u32[]{:S(2)}, u32[]{:S(2)}) collective-permute-start(bf16[32,1792]{1,0:T(8,128)(2,1)S(1)} %get-tuple-element.96), channel_id=1, source_target_pairs={{0,2},{1,9},{2,4},{3,11},{4,6},{5,13},{6,0},{7,15},{8,10},{9,17},{... | collective-permute-start | bytes 344072 | tf_op jit(solution)/shard_map/ppermute | solution.py:37
  550.6 14.3 %collective-permute-start.53 = (bf16[32,1792]{1,0:T(8,128)(2,1)S(1)}, bf16[32,1792]{1,0:T(8,128)(2,1)S(1)}, u32[]{:S(2)}, u32[]{:S(2)}) collective-permute-start(bf16[32,1792]{1,0:T(8,128)(2,1)S(1)} %get-tuple-element.97), channel_id=1, source_target_pairs={{0,6},{1,25},{2,0},{3,27},{4,2},{5,29},{6,4},{7,31},{8,14},{9,1},{... | collective-permute-start | bytes 344072 | tf_op jit(solution)/shard_map/ppermute | solution.py:37
  (33 other events, 317.5 us)
Sparse Core Ops, SparseCore 0:
  304.5 48.7 reduce-scatter.4
  355.8 108.7 reduce-scatter.2

commit v3 on v0

v3 whole, which is shorter than its diff:
```python
import functools

import jax
import jax.numpy as jnp
from jax import lax
from jax.experimental import pallas as pl
from jax.experimental.pallas import tpu as pltpu
from jax.sharding import PartitionSpec as P

SIDE = 4
SEGMENTS = 1 + SIDE
BLOCK = 4
WINDOW = 128
ALIGN = 16
EARLY = (0, 1, 3)
LATE = (2,)
VMEM = 60 * 1024 * 1024


def ep_of(x, y, core):
    return (x * SIDE + y) * 2 + core


def moved(index, ring, step):
    x, y, core = index // (2 * SIDE), index // 2 % SIDE, index % 2
    if (ring == 0) == (core == 0):
        return ep_of(x, (y + step) % SIDE, core)
    return ep_of((x + step) % SIDE, y, core)


def shift_z(value, step):
    return lax.ppermute(value, "grp", [(i, (i + step) % SIDE) for i in range(SIDE)])


def shift_ring(value, ring, step):
    count = 2 * SIDE * SIDE
    return lax.ppermute(value, "ep", [(i, moved(i, ring, step)) for i in range(count)])


def swap_cores(value):
    count = 2 * SIDE * SIDE
    return lax.ppermute(value, "ep", [(i, i ^ 1) for i in range(count)])


def from_all(shift, value):
    return jnp.stack([value, shift(value, -1), shift(value, 2), shift(value, 1)])


def hidden_kernel(capacity, tile, sources, meta, places, gate_hbm, up_hbm, *rest):
    blocks = len(sources)
    count = max(piece for block in sources for piece, _ in block) + 1
    pieces = rest[:count]
    own_out, hot_out, gate, up, gathered, compact, packed, weight_sems, row_sems = rest[-9:]
    rows = pieces[0].shape[2]
    width, hidden = gate.shape
    block_rows = BLOCK * rows
    me, donates, total = meta[0], meta[1] == 1, meta[2]
    offsets, counts, begins = 3, 3 + SEGMENTS, 3 + 2 * SEGMENTS

    def load(block, distance):
        for unit, (piece, place) in enumerate(sources[block]):
            pltpu.make_async_copy(
                pieces[piece].at[place, distance],
                gathered.at[block, pl.ds(unit * rows, rows)],
                row_sems.at[block],
            ).start()

    def arrive(block):
        pltpu.make_async_copy(gathered.at[block], gathered.at[block], row_sems.at[block]).wait()

    def pick(segment, block):
        start = pl.multiple_of(meta[begins + segment * blocks + block], ALIGN)
        place = places[pl.ds(segment * blocks + block, 1), :] - start
        slots = lax.broadcasted_iota(jnp.int32, (WINDOW, block_rows), 0)
        choose = jnp.where(slots == place, 1.0, 0.0).astype(jnp.bfloat16)

        found = jnp.dot(choose, gathered[block], preferred_element_type=jnp.float32).astype(jnp.bfloat16)
        compact[pl.ds(start, ALIGN), :] = compact[pl.ds(start, ALIGN), :] + found[:ALIGN]
        compact[pl.ds(start + ALIGN, WINDOW - ALIGN), :] = found[ALIGN:]

    weights = (
        pltpu.make_async_copy(gate_hbm, gate, weight_sems.at[0]),
        pltpu.make_async_copy(up_hbm, up, weight_sems.at[1]),
    )
    for block in range(blocks):
        load(block, 0)
    for copy in weights:
        copy.start()
    compact[:ALIGN, :] = jnp.zeros((ALIGN, width), jnp.bfloat16)
    for block in range(blocks):
        arrive(block)
        pick(0, block)

    @pl.when(donates)
    def _():
        def group(distance, carry):
            for block in range(blocks):
                pl.when(distance > 0)(functools.partial(arrive, block))
                pick(1 + distance, block)
                pl.when(distance < SIDE - 1)(functools.partial(load, block, distance + 1))
            return carry
        lax.fori_loop(0, SIDE, group, 0)

    for copy in weights:
        copy.wait()

    def serve(t, carry):
        span = pl.ds(pl.multiple_of(t * tile, tile), tile)
        gate_part = jnp.dot(compact[span, :], gate[...], preferred_element_type=jnp.float32)
        up_part = jnp.dot(compact[span, :], up[...], preferred_element_type=jnp.float32)
        packed[span, :] = (jax.nn.silu(gate_part) * up_part).astype(jnp.bfloat16)
        return carry

    lax.fori_loop(0, lax.div(total + tile - 1, tile), serve, 0)

    def unpack(segment, store):
        for t in range(0, capacity, WINDOW):
            begin = pl.multiple_of(meta[offsets + segment] + t, ALIGN)
            live = lax.broadcasted_iota(jnp.int32, (WINDOW, hidden), 0) < meta[counts + segment] - t
            value = packed[pl.ds(begin, WINDOW), :]
            store(pl.ds(t, WINDOW), jnp.where(live, value, jnp.zeros_like(value)))

    def own_store(span, value):
        own_out[span, :] = value

    unpack(0, own_store)
    for distance in range(SIDE):
        group = lax.rem(me + distance, SIDE)

        def hot_store(span, value):
            hot_out[group, span, :] = value

        unpack(1 + distance, hot_store)


def hidden_call(capacity, tile, sources, meta, places, gate, up, pieces, after=()):
    rows = pieces[0].shape[2]
    width, hidden = gate.shape
    blocks = len(sources)
    block_rows = BLOCK * rows
    most = SEGMENTS * capacity + tile
    anywhere = pl.BlockSpec(memory_space=pl.ANY)
    return pl.pallas_call(
        functools.partial(hidden_kernel, capacity, tile, sources),
        in_specs=[pl.BlockSpec(memory_space=pltpu.SMEM), pl.BlockSpec(memory_space=pltpu.VMEM)]
        + [anywhere] * (2 + len(pieces) + len(after)),
        out_specs=[pl.BlockSpec(memory_space=pltpu.VMEM)] * 2,
        out_shape=[
            jax.ShapeDtypeStruct((capacity, hidden), jnp.bfloat16),
            jax.ShapeDtypeStruct((SIDE, capacity, hidden), jnp.bfloat16),
        ],
        scratch_shapes=[
            pltpu.VMEM((width, hidden), jnp.bfloat16),
            pltpu.VMEM((width, hidden), jnp.bfloat16),
            pltpu.VMEM((blocks, block_rows, width), jnp.bfloat16),
            pltpu.VMEM((most, width), jnp.bfloat16),
            pltpu.VMEM((most, hidden), jnp.bfloat16),
            pltpu.SemaphoreType.DMA((2,)),
            pltpu.SemaphoreType.DMA((blocks,)),
        ],
        compiler_params=pltpu.CompilerParams(vmem_limit_bytes=VMEM),
        cost_estimate=pl.CostEstimate(
            flops=SEGMENTS * capacity * width * hidden * 2,
            bytes_accessed=2 * width * hidden * 2 + 4 * blocks * block_rows * width * 2,
            transcendentals=SEGMENTS * capacity * hidden,
        ),
    )(meta, places, gate, up, *pieces, *after)

def tables(member, grp, donates):
    blocks, block_rows = member.shape[1:]
    after = jnp.cumsum(member.reshape(SEGMENTS, -1), axis=1).reshape(member.shape)
    counts = after[:, -1, -1]
    before = jnp.concatenate([jnp.zeros((SEGMENTS, 1), jnp.int32), after[:, :-1, -1]], axis=1)
    serves = jnp.where(jnp.arange(SEGMENTS) == 0, 1, donates)
    room = (counts + ALIGN - 1) // ALIGN * ALIGN * serves
    offsets = jnp.cumsum(room) - room
    begins = offsets[:, None] + before // ALIGN * ALIGN
    places = jnp.where(member == 1, offsets[:, None, None] + after - 1, -1).reshape(SEGMENTS * blocks, block_rows)
    meta = jnp.concatenate([jnp.stack([grp, donates, jnp.sum(room)]), offsets, counts * serves, begins.reshape(-1)])
    return meta.astype(jnp.int32), places, after, before


def combine_kernel(starts, scales, own_early, own_late, hot_early, hot_late, down, copied, theirs, mine, outs, pair):
    early = own_early.shape[0]
    late = own_late.shape[0]
    total = early + late
    block_rows = mine.shape[0] // SIDE

    outs[:early, :] = jnp.dot(own_early[...], down[...], preferred_element_type=jnp.float32).astype(jnp.bfloat16)
    outs[early:total, :] = jnp.dot(own_late[...], down[...], preferred_element_type=jnp.float32).astype(jnp.bfloat16)
    outs[total:total + early, :] = jnp.dot(hot_early[...], copied[...], preferred_element_type=jnp.float32).astype(jnp.bfloat16)
    outs[total + early:, :] = jnp.dot(hot_late[...], copied[...], preferred_element_type=jnp.float32).astype(jnp.bfloat16)

    for out, first in ((theirs, 0), (mine, SIDE)):
        for b in range(SIDE):
            own_start = pl.multiple_of(starts[2 * (first + b)], ALIGN)
            hot_start = pl.multiple_of(starts[2 * (first + b) + 1], ALIGN)
            pair[first + b, :WINDOW, :] = outs[pl.ds(own_start, WINDOW), :]
            pair[first + b, WINDOW:, :] = outs[pl.ds(total + hot_start, WINDOW), :]
            scale = scales[(first + b) * block_rows:(first + b + 1) * block_rows, :]
            value = jnp.dot(scale, pair[first + b], preferred_element_type=jnp.float32)
            out[b * block_rows:(b + 1) * block_rows, :] = value.astype(jnp.bfloat16)


def combine_call(part, parts, starts, scales, own_early, own_late, hot_early, hot_late, down, copied):
    hidden = down.shape[0]
    width = down.shape[1] // parts
    wide = width // 2 if width % 256 == 0 else width
    rows = scales.shape[0]
    whole = pl.BlockSpec(memory_space=pltpu.VMEM)
    offset = part * (width // wide)
    column = pl.BlockSpec((hidden, wide), lambda n: (0, offset + n))
    result = pl.BlockSpec((rows // 2, wide), lambda n: (0, n))
    slots = 2 * (own_early.shape[0] + own_late.shape[0])
    return pl.pallas_call(
        combine_kernel,
        grid=(width // wide,),
        in_specs=[pl.BlockSpec(memory_space=pltpu.SMEM)] + [whole] * 5 + [column, column],
        out_specs=[result, result],
        out_shape=[jax.ShapeDtypeStruct((rows // 2, width), jnp.bfloat16)] * 2,
        scratch_shapes=[pltpu.VMEM((slots, wide), jnp.bfloat16), pltpu.VMEM((2 * SIDE, 2 * WINDOW, wide), jnp.bfloat16)],
        compiler_params=pltpu.CompilerParams(vmem_limit_bytes=VMEM),
        cost_estimate=pl.CostEstimate(
            flops=2 * slots * hidden * width + 4 * rows * WINDOW * width,
            bytes_accessed=4 * hidden * width + 2 * rows * width,
            transcendentals=0,
        ),
    )(starts, scales, own_early, own_late, hot_early, hot_late, down, copied)


def add(*values):
    return sum(v.astype(jnp.float32) for v in values).astype(jnp.bfloat16)


def sum_to_owners(theirs, mine, rows):
    width = mine.shape[1]
    total = add(mine, swap_cores(theirs)).reshape(SIDE, SIDE, rows, width)
    for ring, shape in ((1, (SIDE, rows, width)), (0, (rows, width))):
        cut = shape[0] // 2
        ahead = shift_ring(total[2, :cut], ring, 1)
        behind = shift_ring(total[2, cut:], ring, -1)
        forward = jnp.concatenate([add(total[1, :cut], ahead), total[1, cut:]], axis=0)
        backward = jnp.concatenate([total[3, :cut], add(total[3, cut:], behind)], axis=0)
        total = add(total[0], shift_ring(forward, ring, 1), shift_ring(backward, ring, -1))
    return total


def local(tokens, route_ids, route_gates, w_gate, w_up, w_down, hot_source):
    n_ep = lax.axis_size("ep")
    grp, ep = lax.axis_index("grp"), lax.axis_index("ep")
    core, x, y = lax.rem(ep, 2), ep // (2 * SIDE), lax.rem(ep // 2, SIDE)
    rows = tokens[0]
    row_count, width = rows.shape
    picks = route_ids.shape[2]
    cap = row_count * picks // n_ep
    donor = hot_source[0]
    own_gate, own_up, own_down = w_gate[0, 0], w_up[0, 0], w_down[0, 0]

    info = jnp.concatenate([route_ids[0].astype(jnp.bfloat16), route_gates[0]], axis=1).T
    info = info.reshape(-1, 128)
    info = from_all(shift_z, info)
    info = from_all(lambda value, step: shift_ring(value, 0, step), info)
    info = from_all(lambda value, step: shift_ring(value, 1, step), info)
    info = jnp.stack([info, swap_cores(info)])
    info = info.reshape(2 * SIDE, SIDE, SIDE, 2 * picks, row_count)

    below, above = shift_z(rows, 1), shift_z(rows, -1)
    cut = row_count // 2
    far = (shift_z(below[:cut], 1), shift_z(above[cut:], -1))
    unit = jnp.stack([rows, above, jnp.concatenate(far, axis=0), below])
    gives = (donor == grp) & (unit[2, 0, 0] == unit[2, 0, 0])
    copied = lax.psum(jnp.where(gives, own_down, jnp.zeros_like(own_down)), "grp")
    below, above = shift_ring(unit, 0, 1), shift_ring(unit, 0, -1)
    far = (shift_ring(below[:2], 0, 1), shift_ring(above[2:], 0, -1))
    low, high = jnp.stack([unit, above]), jnp.stack([jnp.concatenate(far, axis=0), below])
    low_below, high_above = shift_ring(low, 1, 1), shift_ring(high, 1, -1)
    high_below, low_above = shift_ring(high, 1, 1), shift_ring(low, 1, -1)
    low_far, high_far = shift_ring(low_below, 1, 1), shift_ring(high_above, 1, -1)
    early = [low, high, low_above, high_above, low_below, high_below]
    early = early + [swap_cores(piece) for piece in early]
    late = [low_far, high_far]
    late = late + [swap_cores(piece) for piece in late]

    order = [(other, second) for seconds in (EARLY, LATE) for other in (0, 1) for second in seconds]
    info = jnp.stack([info[other * SIDE + second] for other, second in order])
    ids = info[:, :, :, :picks].astype(jnp.int32)
    gates = info[:, :, :, picks:].astype(jnp.float32)
    is_own, is_hot = ids[:, :, 0] == ep, ids == ep + n_ep
    block_rows = BLOCK * row_count
    member = jnp.concatenate([jnp.any(is_own, axis=2)[:, :, None], jnp.any(is_hot, axis=3)], axis=2)
    member = member.transpose(2, 0, 1, 3).reshape(SEGMENTS, len(order), block_rows).astype(jnp.int32)
    own_scale = jnp.sum(jnp.where(is_own, gates[:, :, 0], 0.0), axis=2).reshape(len(order), block_rows)
    hot_scale = jnp.sum(jnp.where(is_hot[:, :, 0], gates[:, :, 0], 0.0), axis=2).reshape(len(order), block_rows)
    donates = (donor == grp).astype(jnp.int32)

    first_late = 2 * len(EARLY)
    early_slots, late_slots = first_late * BLOCK * cap, 2 * len(LATE) * BLOCK * cap
    early_meta, early_places, early_after, early_before = tables(member[:, :first_late], grp, donates)
    late_meta, late_places, late_after, late_before = tables(member[:, first_late:], grp, donates)
    piece_of = {0: 0, 1: 2, 3: 4}
    early_sources = [
        [(6 * other + piece_of[second] + first // 2, first % 2) for first in range(SIDE)]
        for other, second in order[:first_late]
    ]
    late_sources = [[(2 * other + first // 2, first % 2) for first in range(SIDE)] for other, _ in order[first_late:]]

    def sent_back(hot):
        return lax.psum_scatter(hot.reshape(-1, hot.shape[2]), "grp", tiled=True)

    own_early, hot_early = hidden_call(
        early_slots, 256, early_sources, early_meta, early_places, own_gate, own_up, early
    )
    own_late, hot_late = hidden_call(
        late_slots, 128, late_sources, late_meta, late_places, own_gate, own_up, late, after=(own_early,)
    )
    hot_early, hot_late = sent_back(hot_early), sent_back(hot_late)

    after = jnp.concatenate([early_after[:2], late_after[:2] + early_slots], axis=1)
    before = jnp.concatenate([early_before[:2], late_before[:2] + early_slots], axis=1)
    wanted = [order.index((other, second)) for other in (1, 0) for second in range(SIDE)]
    take = lambda value: jnp.stack([value[:, index] for index in wanted], axis=1)
    starts = take(jnp.minimum(before // ALIGN * ALIGN, early_slots + late_slots - WINDOW))
    slots = jnp.arange(WINDOW, dtype=jnp.int32)
    chosen = (take(after) - 1 - starts[:, :, None])[..., None] == slots
    scale = take(jnp.stack([own_scale, hot_scale]))[..., None]
    scales = jnp.where(chosen, scale, 0.0).astype(jnp.bfloat16)
    scales = jnp.concatenate([scales[0], scales[1]], axis=-1).reshape(len(order) * block_rows, 2 * WINDOW)
    starts = starts.T.reshape(-1)

    parts = 2
    results = []
    for part in range(parts):
        theirs, mine = combine_call(
            part, parts, starts, scales, own_early, own_late, hot_early, hot_late, own_down, copied
        )
        results.append(sum_to_owners(theirs, mine, row_count))
    return jnp.concatenate(results, axis=1)[None]


def solution(mesh):
    placed = (
        P("grp", "ep", None),
        P("grp", "ep", None),
        P("grp", "ep", None),
        P("grp", "ep", None, None),
        P("grp", "ep", None, None),
        P("grp", "ep", None, None),
        P("ep"),
    )
    return jax.shard_map(
        local, mesh=mesh, in_specs=placed, out_specs=P("grp", "ep", None), check_vma=False
    )
```

time: 586 us -> 478 us (0.82)
  waiting for transfers between devices: 347 us -> 255 us
  blocking collectives: 91.7 us -> 0 us
  Pallas kernels: 0 us -> 86.3 us
  starting transfers between devices: 7.34 us -> 74 us
  matrix products: 53.8 us -> 0 us
  local copies, waits for them, and re-layouts: 38.3 us -> 8.21 us
    psum x1, waiting for transfers between devices: 247 us -> 0.01 us  [local(): lax.psum(jnp.where(gives, own_down, jnp.zeros_like(own_down)), 'grp')]
    ppermute x0 -> x50, waiting for transfers between devices: none -> 193 us  [the longest x32 168 us: shift_ring(): lax.ppermute(value, 'ep', [(i, moved(i, ring, step)) for i in range(count)])]
    all_to_all x1 -> x0, waiting for transfers between devices: 99.5 us -> none  [local(): lax.all_to_all(outbox.reshape(2, devices, capacity, feature_count), 'ep',...]
    all_to_all x1 -> x0, blocking collectives: 91.7 us -> none  [local(): lax.all_to_all(outgoing, 'ep', split_axis=1, concat_axis=1, tiled=True)]
    pallas_call x0 -> x4, Pallas kernels: none -> 86.3 us  [the longest x2 62.5 us: hidden_call(): pl.pallas_call(functools.partial(hidden_kernel, capacity, tile, sources),...]
    ppermute x0 -> x50, starting transfers between devices: none -> 73.8 us  [the longest x32 56.5 us: shift_ring(): lax.ppermute(value, 'ep', [(i, moved(i, ring, step)) for i in range(count)])]
    reduce_scatter x0 -> x2, waiting for transfers between devices: none -> 61.9 us  [sent_back(): return lax.psum_scatter(hot.reshape(-1, hot.shape[2]), 'grp', tiled=True)]
    dot_general x5 -> x0, matrix products: 53.8 us -> none  [the longest x2 33.9 us: expert_apply(): jnp.dot(hidden, weight_down, preferred_element_type=jnp.float32)]
  transfers between devices with their start and end apart: 2 -> 53, of which waited for: 2 -> 29; matrix products, arithmetic and copies ran while one was open for 8% -> 7% of each run, Pallas kernels for 0% -> 16%
where the time goes in v3:
time: 478 us; the launch traced here: 469 us
  waiting for transfers between devices  255 us (53%)
  Pallas kernels  86.3 us (18%)
  starting transfers between devices  74 us (15%)
  other arithmetic  28.6 us (6%)
  between operations  16.1 us (3%)
  local copies, waits for them, and re-layouts  8.21 us (2%)
    ppermute x32, waiting for transfers between devices, shift_ring(): lax.ppermute(value, 'ep', [(i, moved(i, ring, step)) for i in range(count)])  168 us
    pallas_call x2, Pallas kernels, hidden_call(): pl.pallas_call(functools.partial(hidden_kernel, capacity, tile, sources),...  62.5 us
    reduce_scatter x2, waiting for transfers between devices, sent_back(): return lax.psum_scatter(hot.reshape(-1, hot.shape[2]), 'grp', tiled=True)  61.9 us
    ppermute x32, starting transfers between devices, shift_ring(): lax.ppermute(value, 'ep', [(i, moved(i, ring, step)) for i in range(count)])  56.5 us
    ppermute x7, waiting for transfers between devices, shift_z(): lax.ppermute(value, 'grp', [(i, (i + step) % SIDE) for i in range(SIDE)])  24.2 us
    pallas_call x2, Pallas kernels, combine_call(): pl.pallas_call(combine_kernel, grid=(width // wide,), in_specs=[pl.BlockS...  23.8 us
    ppermute x7, starting transfers between devices, shift_z(): lax.ppermute(value, 'grp', [(i, (i + step) % SIDE) for i in range(SIDE)])  13.1 us
  transfers between devices with their start and end apart: 53, of which 29 were waited for; matrix products, arithmetic and copies ran while one was open for 7% of the time, Pallas kernels for 16%

profile of v3, /device:TPU:0, one launch (start us, length us, event | category | flops | bytes accessed | tf_op | source)
XLA Modules:
  0.0 468.6 jit_solution(8561777742679734538)
XLA Ops:
  10.7 10.7 %collective-permute-done.11 = bf16[64,3584]{1,0:T(8,128)(2,1)S(1)} collective-permute-done((bf16[64,3584]{1,0:T(8,128)(2,1)}, bf16[64,3584]{1,0:T(8,128)(2,1)S(1)}, u32[]{:S(2)}, u32[]{:S(2)}) %collective-permute-start.11) | collective-permute-done | bytes 458784 | tf_op jit(solution)/shard_map/ppermute | solution.py:32
  21.5 3.3 collective-permute-start.13
  24.8 4.7 collective-permute-done.12
  34.1 21.2 %collective-permute-done.15 = bf16[4,64,3584]{2,1,0:T(8,128)(2,1)S(1)} collective-permute-done((bf16[4,64,3584]{2,1,0:T(8,128)(2,1)S(1)}, bf16[4,64,3584]{2,1,0:T(8,128)(2,1)S(1)}, u32[]{:S(2)}, u32[]{:S(2)}) %collective-permute-start.15) | collective-permute-done | bytes 1835040 | tf_op jit(solution)/shard_map/ppermute | solution.py:37
  55.9 2.9 collective-permute-start.17
  64.3 13.8 %collective-permute-done.16 = bf16[2,64,3584]{2,1,0:T(8,128)(2,1)S(1)} collective-permute-done((bf16[2,64,3584]{2,1,0:T(8,128)(2,1)S(1)}, bf16[2,64,3584]{2,1,0:T(8,128)(2,1)S(1)}, u32[]{:S(2)}, u32[]{:S(2)}) %collective-permute-start.16) | collective-permute-done | bytes 917536 | tf_op jit(solution)/shard_map/ppermute | solution.py:37
  80.5 4.5 collective-permute-start.19
  85.0 3.1 collective-permute-start
  91.2 3.4 collective-permute-done.1
  95.4 4.1 collective-permute-done.2
  99.6 3.5 collective-permute-start.3
  106.3 3.3 collective-permute-done.4
  110.7 4.3 collective-permute-done.5
  116.0 29.5 %collective-permute-done.6 = bf16[4,4,8,128]{3,2,1,0:T(8,128)(2,1)S(1)} collective-permute-done((bf16[4,4,8,128]{3,2,1,0:T(8,128)(2,1)S(1)}, bf16[4,4,8,128]{3,2,1,0:T(8,128)(2,1)S(1)}, u32[]{:S(2)}, u32[]{:S(2)}) %collective-permute-start.6) | collective-permute-done | bytes 32800 | tf_op jit(solution)/shard_map/ppermute | solution.py:37
  145.5 2.7 collective-permute-start.7
  148.2 2.7 collective-permute-done.7
  152.4 3.8 collective-permute-done.8
  165.6 6.6 %broadcast_select_fusion = bf16[1024,3584]{1,0:T(8,128)(2,1)} fusion(pred[]{:T(512)S(6)} %and.90, bf16[1,1,1024,3584]{3,2,1,0:T(8,128)(2,1)} %param.12), kind=kLoop, calls=%fused_computation.2 | loop fusion | flops 3670016 | bytes 14680065 | tf_op jit(solution)/shard_map/jit(_where)/select_n | solution.py:272
  172.9 30.4 %collective-permute-done.21.rest_5_ = bf16[2,4,64,3584]{3,2,1,0:T(8,128)(2,1)} collective-permute-done((bf16[2,4,64,3584]{3,2,1,0:T(8,128)(2,1)}, bf16[2,4,64,3584]{3,2,1,0:T(8,128)(2,1)}, u32[]{:S(2)}, u32[]{:S(2)}) %collective-permute-start.21) | collective-permute-done | bytes 3670048 | tf_op jit(solution)/shard_map/ppermute | solution.py:37
  206.8 35.8 %collective-permute-done.28.rest_0_ = bf16[2,4,64,3584]{3,2,1,0:T(8,128)(2,1)} collective-permute-done((bf16[2,4,64,3584]{3,2,1,0:T(8,128)(2,1)}, bf16[2,4,64,3584]{3,2,1,0:T(8,128)(2,1)}, u32[]{:S(2)}, u32[]{:S(2)}) %collective-permute-start.28) | collective-permute-done | bytes 3670048 | tf_op jit(solution)/shard_map/ppermute | solution.py:37
  252.4 42.6 %shard_map.73 = (bf16[384,1024]{1,0:T(8,128)(2,1)}, bf16[4,384,1024]{2,1,0:T(8,128)(2,1)}) custom-call(s32[43]{0:T(128)} %concatenate.74.meta, s32[30,256]{1,0:T(8,128)} %reshape.343.places, bf16[3584,1024]{1,0:T(8,128)(2,1)} %bitcast.175, bf16[3584,1024]{1,0:T(8,128)(2,1)} %bitcast.177, bf16[2,4,64,3584]{3,2,1,0:T(8,128)(2,1)} %pad_maximum_fusion.rest_0_, ...), custom_call_target="tpu_custom_call" | custom-call | flops 14092861440 | bytes 58720256 | tf_op jit(solution)/shard_map/pallas_call | solution.py:143
  295.0 19.9 %shard_map.74 = (bf16[128,1024]{1,0:T(8,128)(2,1)}, bf16[4,128,1024]{2,1,0:T(8,128)(2,1)}) custom-call(s32[23]{0:T(128)} %concatenate.77.meta, s32[10,256]{1,0:T(8,128)} %reshape.347.places, bf16[3584,1024]{1,0:T(8,128)(2,1)} %bitcast.176, bf16[3584,1024]{1,0:T(8,128)(2,1)} %bitcast.178, bf16[2,4,64,3584]{3,2,1,0:T(8,128)(2,1)} %collective-permute-done.28.rest_0_, ...), custom_call_target="tpu_custom_call" | custom-call | flops 4697620480 | bytes 29360128 | tf_op jit(solution)/shard_map/pallas_call | solution.py:143
  319.9 21.3 %reduce-scatter.5.cloned.1.call-done.hot_late = bf16[128,1024]{1,0:T(8,128)(2,1)} async-done(((bf16[512,1024]{1,0:T(8,128)(2,1)}), bf16[128,1024]{1,0:T(8,128)(2,1)}) %reduce-scatter.5.cloned.1.call-update) | async-done | bytes 262160 | tf_op jit(solution)/shard_map/reduce_scatter | solution.py:308
  341.2 40.6 %reduce-scatter.3.cloned.1.call-done.hot_early = bf16[384,1024]{1,0:T(8,128)(2,1)} async-done(((bf16[1536,1024]{1,0:T(8,128)(2,1)}), bf16[384,1024]{1,0:T(8,128)(2,1)}) %reduce-scatter.3.cloned.1.call-update) | async-done | bytes 786448 | tf_op jit(solution)/shard_map/reduce_scatter | solution.py:308
  381.7 11.8 %shard_map.75 = (bf16[1024,1792]{1,0:T(8,128)(2,1)}, bf16[1024,1792]{1,0:T(8,128)(2,1)}) custom-call(s32[16]{0:T(128)} %reshape.339.starts, bf16[2048,256]{1,0:T(8,128)(2,1)} %pad_maximum_fusion.3.scales, bf16[384,1024]{1,0:T(8,128)(2,1)} %get-tuple-element.13.rest_4_.own_early, bf16[128,1024]{1,0:T(8,128)(2,1)} %get-tuple-element.14.own_late, ...), custom_call_target="tpu_custom_call" | custom-call | flops 5637144576 | bytes 14680064 | tf_op jit(solution)/shard_map/pallas_call | solution.py:215
  393.7 12.0 %shard_map.76 = (bf16[1024,1792]{1,0:T(8,128)(2,1)}, bf16[1024,1792]{1,0:T(8,128)(2,1)}) custom-call(s32[16]{0:T(128)} %reshape.339.starts, bf16[2048,256]{1,0:T(8,128)(2,1)} %pad_maximum_fusion.3.scales, bf16[384,1024]{1,0:T(8,128)(2,1)} %get-tuple-element.13.rest_4_.own_early, bf16[128,1024]{1,0:T(8,128)(2,1)} %get-tuple-element.14.own_late, ...), custom_call_target="tpu_custom_call" | custom-call | flops 5637144576 | bytes 14680064 | tf_op jit(solution)/shard_map/pallas_call | solution.py:215
  406.5 2.9 add_convert_fusion.1
  428.4 6.3 %collective-permute-done.34 = bf16[4,64,1792]{2,1,0:T(8,128)(2,1)S(1)} collective-permute-done((bf16[4,64,1792]{2,1,0:T(8,128)(2,1)S(1)}, bf16[4,64,1792]{2,1,0:T(8,128)(2,1)S(1)}, u32[]{:S(2)}, u32[]{:S(2)}) %collective-permute-start.34) | collective-permute-done | bytes 917536 | tf_op jit(solution)/shard_map/ppermute | solution.py:37
  438.8 7.0 %collective-permute-done.43 = bf16[4,64,1792]{2,1,0:T(8,128)(2,1)S(1)} collective-permute-done((bf16[4,64,1792]{2,1,0:T(8,128)(2,1)S(1)}, bf16[4,64,1792]{2,1,0:T(8,128)(2,1)S(1)}, u32[]{:S(2)}, u32[]{:S(2)}) %collective-permute-start.43) | collective-permute-done | bytes 917536 | tf_op jit(solution)/shard_map/ppermute | solution.py:37
  450.3 3.0 collective-permute-start.40
  454.6 2.3 collective-permute-start.49
  457.3 3.4 collective-permute-done.47
  (214 shorter events, 85.4 us)
Async XLA Ops:
  6.5 313.3 %all-reduce.4.cloned.1.call-start = ((), (), s32[]{:S(2)}) async-start(), calls=%async_computation.4 | async-start | bytes 14680064 | tf_op jit(solution)/shard_map/psum | solution.py:272
  6.5 14.8 %collective-permute-start.11 = (bf16[64,3584]{1,0:T(8,128)(2,1)}, bf16[64,3584]{1,0:T(8,128)(2,1)S(1)}, u32[]{:S(2)}, u32[]{:S(2)}) collective-permute-start(bf16[64,3584]{1,0:T(8,128)(2,1)} %bitcast.196), channel_id=1, source_target_pairs={{0,32},{32,64},{64,96},{96,0},{1,33},{33,65},{65,97},{97,1},{2,34}... | collective-permute-start | bytes 1376264 | tf_op jit(solution)/shard_map/ppermute | solution.py:32
  8.5 13.0 %collective-permute-start.10 = (bf16[64,3584]{1,0:T(8,128)(2,1)}, bf16[64,3584]{1,0:T(8,128)(2,1)S(1)}, u32[]{:S(2)}, u32[]{:S(2)}) collective-permute-start(bf16[64,3584]{1,0:T(8,128)(2,1)} %bitcast.197), channel_id=1, source_target_pairs={{0,96},{32,0},{64,32},{96,64},{1,97},{33,1},{65,33},{97,65},{2,98}... | collective-permute-start | bytes 1376264 | tf_op jit(solution)/shard_map/ppermute | solution.py:32
  30.8 24.5 %collective-permute-start.15 = (bf16[4,64,3584]{2,1,0:T(8,128)(2,1)S(1)}, bf16[4,64,3584]{2,1,0:T(8,128)(2,1)S(1)}, u32[]{:S(2)}, u32[]{:S(2)}) collective-permute-start(bf16[4,64,3584]{2,1,0:T(8,128)(2,1)S(1)} %get-tuple-element.47), channel_id=1, source_target_pairs={{0,2},{1,9},{2,4},{3,11},{4,6},{5,13},{6,0},{7,15},{8,10},{9,17},{... | collective-permute-start | bytes 5505032 | tf_op jit(solution)/shard_map/ppermute | solution.py:37
  32.5 23.4 %collective-permute-start.14 = (bf16[4,64,3584]{2,1,0:T(8,128)(2,1)S(1)}, bf16[4,64,3584]{2,1,0:T(8,128)(2,1)S(1)}, u32[]{:S(2)}, u32[]{:S(2)}) collective-permute-start(bf16[4,64,3584]{2,1,0:T(8,128)(2,1)S(1)} %get-tuple-element.47), channel_id=1, source_target_pairs={{0,6},{1,25},{2,0},{3,27},{4,2},{5,29},{6,4},{7,31},{8,14},{9,1},{... | collective-permute-start | bytes 5505032 | tf_op jit(solution)/shard_map/ppermute | solution.py:37
  55.4 22.6 %collective-permute-start.16 = (bf16[2,64,3584]{2,1,0:T(8,128)(2,1)S(1)}, bf16[2,64,3584]{2,1,0:T(8,128)(2,1)S(1)}, u32[]{:S(2)}, u32[]{:S(2)}) collective-permute-start(bf16[2,64,3584]{2,1,0:T(8,128)(2,1)S(1)} %slice.370), channel_id=1, source_target_pairs={{0,2},{1,9},{2,4},{3,11},{4,6},{5,13},{6,0},{7,15},{8,10},{9,17},{... | collective-permute-start | bytes 2752520 | tf_op jit(solution)/shard_map/ppermute | solution.py:37
  55.9 22.3 %collective-permute-start.17 = (bf16[2,64,3584]{2,1,0:T(8,128)(2,1)S(1)}, bf16[2,64,3584]{2,1,0:T(8,128)(2,1)S(1)}, u32[]{:S(2)}, u32[]{:S(2)}) collective-permute-start(bf16[2,64,3584]{2,1,0:T(8,128)(2,1)S(1)} %slice.371), channel_id=1, source_target_pairs={{0,6},{1,25},{2,0},{3,27},{4,2},{5,29},{6,4},{7,31},{8,14},{9,1},{... | collective-permute-start | bytes 2752520 | tf_op jit(solution)/shard_map/ppermute | solution.py:37
  61.0 98.3 %collective-permute-start.20 = (bf16[2,4,64,3584]{3,2,1,0:T(8,128)(2,1)}, bf16[2,4,64,3584]{3,2,1,0:T(8,128)(2,1)}, u32[]{:S(2)}, u32[]{:S(2)}) collective-permute-start(bf16[2,4,64,3584]{3,2,1,0:T(8,128)(2,1)} %pad_maximum_fusion.rest_0_), channel_id=1, source_target_pairs={{0,8},{1,3},{2,10},{3,5},{4,12},{5,7},{6,14},{7,1},{8,16},{9,11},{... | collective-permute-start | bytes 11010056 | tf_op jit(solution)/shard_map/ppermute | solution.py:37
  62.5 96.8 %collective-permute-start.18 = (bf16[2,4,64,3584]{3,2,1,0:T(8,128)(2,1)}, bf16[2,4,64,3584]{3,2,1,0:T(8,128)(2,1)}, u32[]{:S(2)}, u32[]{:S(2)}) collective-permute-start(bf16[2,4,64,3584]{3,2,1,0:T(8,128)(2,1)} %pad_maximum_fusion.rest_0_), channel_id=1, source_target_pairs={{0,24},{1,7},{2,26},{3,1},{4,28},{5,3},{6,30},{7,5},{8,0},{9,15},{... | collective-permute-start | bytes 11010056 | tf_op jit(solution)/shard_map/ppermute | solution.py:37
  64.3 98.0 %collective-permute-start.22 = (bf16[2,4,64,3584]{3,2,1,0:T(8,128)(2,1)}, bf16[2,4,64,3584]{3,2,1,0:T(8,128)(2,1)}, u32[]{:S(2)}, u32[]{:S(2)}) collective-permute-start(bf16[2,4,64,3584]{3,2,1,0:T(8,128)(2,1)} %pad_maximum_fusion.rest_0_), channel_id=1, source_target_pairs={{0,1},{1,0},{2,3},{3,2},{4,5},{5,4},{6,7},{7,6},{8,9},{9,8},{10,11... | collective-permute-start | bytes 11010056 | tf_op jit(solution)/shard_map/ppermute | solution.py:42
  80.5 83.4 %collective-permute-start.19 = (bf16[2,4,64,3584]{3,2,1,0:T(8,128)(2,1)}, bf16[2,4,64,3584]{3,2,1,0:T(8,128)(2,1)}, u32[]{:S(2)}, u32[]{:S(2)}) collective-permute-start(bf16[2,4,64,3584]{3,2,1,0:T(8,128)(2,1)} %pad_maximum_fusion.1.rest_1_), channel_id=1, source_target_pairs={{0,24},{1,7},{2,26},{3,1},{4,28},{5,3},{6,30},{7,5},{8,0},{9,15},{... | collective-permute-start | bytes 11010056 | tf_op jit(solution)/shard_map/ppermute | solution.py:37
  115.1 30.4 %collective-permute-start.6 = (bf16[4,4,8,128]{3,2,1,0:T(8,128)(2,1)S(1)}, bf16[4,4,8,128]{3,2,1,0:T(8,128)(2,1)S(1)}, u32[]{:S(2)}, u32[]{:S(2)}) collective-permute-start(bf16[4,4,8,128]{3,2,1,0:T(8,128)(2,1)S(1)} %get-tuple-element.65), channel_id=1, source_target_pairs={{0,24},{1,7},{2,26},{3,1},{4,28},{5,3},{6,30},{7,5},{8,0},{9,15},{... | collective-permute-start | bytes 98312 | tf_op jit(solution)/shard_map/ppermute | solution.py:37
  158.8 44.4 %collective-permute-start.21 = (bf16[2,4,64,3584]{3,2,1,0:T(8,128)(2,1)}, bf16[2,4,64,3584]{3,2,1,0:T(8,128)(2,1)}, u32[]{:S(2)}, u32[]{:S(2)}) collective-permute-start(bf16[2,4,64,3584]{3,2,1,0:T(8,128)(2,1)} %pad_maximum_fusion.1.rest_1_), channel_id=1, source_target_pairs={{0,8},{1,3},{2,10},{3,5},{4,12},{5,7},{6,14},{7,1},{8,16},{9,11},{... | collective-permute-start | bytes 11010056 | tf_op jit(solution)/shard_map/ppermute | solution.py:37
  159.3 43.9 %collective-permute-start.23 = (bf16[2,4,64,3584]{3,2,1,0:T(8,128)(2,1)}, bf16[2,4,64,3584]{3,2,1,0:T(8,128)(2,1)}, u32[]{:S(2)}, u32[]{:S(2)}) collective-permute-start(bf16[2,4,64,3584]{3,2,1,0:T(8,128)(2,1)} %pad_maximum_fusion.1.rest_1_), channel_id=1, source_target_pairs={{0,1},{1,0},{2,3},{3,2},{4,5},{5,4},{6,7},{7,6},{8,9},{9,8},{10,11... | collective-permute-start | bytes 11010056 | tf_op jit(solution)/shard_map/ppermute | solution.py:42
  159.3 44.4 %collective-permute-start.26 = (bf16[2,4,64,3584]{3,2,1,0:T(8,128)(2,1)}, bf16[2,4,64,3584]{3,2,1,0:T(8,128)(2,1)}, u32[]{:S(2)}, u32[]{:S(2)}) collective-permute-start(bf16[2,4,64,3584]{3,2,1,0:T(8,128)(2,1)} %collective-permute-done.20.rest_4_), channel_id=1, source_target_pairs={{0,1},{1,0},{2,3},{3,2},{4,5},{5,4},{6,7},{7,6},{8,9},{9,8},{10,11... | collective-permute-start | bytes 11010056 | tf_op jit(solution)/shard_map/ppermute | solution.py:42
  162.3 80.3 %collective-permute-start.28 = (bf16[2,4,64,3584]{3,2,1,0:T(8,128)(2,1)}, bf16[2,4,64,3584]{3,2,1,0:T(8,128)(2,1)}, u32[]{:S(2)}, u32[]{:S(2)}) collective-permute-start(bf16[2,4,64,3584]{3,2,1,0:T(8,128)(2,1)} %collective-permute-done.20.rest_4_), channel_id=1, source_target_pairs={{0,8},{1,3},{2,10},{3,5},{4,12},{5,7},{6,14},{7,1},{8,16},{9,11},{... | collective-permute-start | bytes 11010056 | tf_op jit(solution)/shard_map/ppermute | solution.py:37
  163.8 78.7 %collective-permute-start.29 = (bf16[2,4,64,3584]{3,2,1,0:T(8,128)(2,1)}, bf16[2,4,64,3584]{3,2,1,0:T(8,128)(2,1)}, u32[]{:S(2)}, u32[]{:S(2)}) collective-permute-start(bf16[2,4,64,3584]{3,2,1,0:T(8,128)(2,1)} %collective-permute-done.19.rest_3_), channel_id=1, source_target_pairs={{0,24},{1,7},{2,26},{3,1},{4,28},{5,3},{6,30},{7,5},{8,0},{9,15},{... | collective-permute-start | bytes 11010056 | tf_op jit(solution)/shard_map/ppermute | solution.py:37
  172.2 168.9 %reduce-scatter.5.cloned.1.call-start = ((), (), s32[]{:S(2)}) async-start(), calls=%async_computation.3 | async-start | bytes 1310720 | tf_op jit(solution)/shard_map/reduce_scatter | solution.py:308
  203.3 49.1 %collective-permute-start.24 = (bf16[2,4,64,3584]{3,2,1,0:T(8,128)(2,1)}, bf16[2,4,64,3584]{3,2,1,0:T(8,128)(2,1)}, u32[]{:S(2)}, u32[]{:S(2)}) collective-permute-start(bf16[2,4,64,3584]{3,2,1,0:T(8,128)(2,1)} %collective-permute-done.18.rest_2_), channel_id=1, source_target_pairs={{0,1},{1,0},{2,3},{3,2},{4,5},{5,4},{6,7},{7,6},{8,9},{9,8},{10,11... | collective-permute-start | bytes 11010056 | tf_op jit(solution)/shard_map/ppermute | solution.py:42
  203.3 49.1 %collective-permute-start.25 = (bf16[2,4,64,3584]{3,2,1,0:T(8,128)(2,1)}, bf16[2,4,64,3584]{3,2,1,0:T(8,128)(2,1)}, u32[]{:S(2)}, u32[]{:S(2)}) collective-permute-start(bf16[2,4,64,3584]{3,2,1,0:T(8,128)(2,1)} %collective-permute-done.19.rest_3_), channel_id=1, source_target_pairs={{0,1},{1,0},{2,3},{3,2},{4,5},{5,4},{6,7},{7,6},{8,9},{9,8},{10,11... | collective-permute-start | bytes 11010056 | tf_op jit(solution)/shard_map/ppermute | solution.py:42
  203.8 48.6 %collective-permute-start.27 = (bf16[2,4,64,3584]{3,2,1,0:T(8,128)(2,1)}, bf16[2,4,64,3584]{3,2,1,0:T(8,128)(2,1)}, u32[]{:S(2)}, u32[]{:S(2)}) collective-permute-start(bf16[2,4,64,3584]{3,2,1,0:T(8,128)(2,1)} %collective-permute-done.21.rest_5_), channel_id=1, source_target_pairs={{0,1},{1,0},{2,3},{3,2},{4,5},{5,4},{6,7},{7,6},{8,9},{9,8},{10,11... | collective-permute-start | bytes 11010056 | tf_op jit(solution)/shard_map/ppermute | solution.py:42
  242.6 52.4 %collective-permute-start.30 = (bf16[2,4,64,3584]{3,2,1,0:T(8,128)(2,1)}, bf16[2,4,64,3584]{3,2,1,0:T(8,128)(2,1)}, u32[]{:S(2)}, u32[]{:S(2)}) collective-permute-start(bf16[2,4,64,3584]{3,2,1,0:T(8,128)(2,1)} %collective-permute-done.28.rest_0_), channel_id=1, source_target_pairs={{0,1},{1,0},{2,3},{3,2},{4,5},{5,4},{6,7},{7,6},{8,9},{9,8},{10,11... | collective-permute-start | bytes 11010056 | tf_op jit(solution)/shard_map/ppermute | solution.py:42
  242.6 52.4 %collective-permute-start.31 = (bf16[2,4,64,3584]{3,2,1,0:T(8,128)(2,1)}, bf16[2,4,64,3584]{3,2,1,0:T(8,128)(2,1)}, u32[]{:S(2)}, u32[]{:S(2)}) collective-permute-start(bf16[2,4,64,3584]{3,2,1,0:T(8,128)(2,1)} %collective-permute-done.29.rest_1_), channel_id=1, source_target_pairs={{0,1},{1,0},{2,3},{3,2},{4,5},{5,4},{6,7},{7,6},{8,9},{9,8},{10,11... | collective-permute-start | bytes 11010056 | tf_op jit(solution)/shard_map/ppermute | solution.py:42
  314.9 66.8 %reduce-scatter.3.cloned.1.call-start = ((), (), s32[]{:S(2)}) async-start(), calls=%async_computation.2 | async-start | bytes 3932160 | tf_op jit(solution)/shard_map/reduce_scatter | solution.py:308
  393.6 12.9 %collective-permute-start.32 = (bf16[1024,1792]{1,0:T(8,128)(2,1)}, bf16[1024,1792]{1,0:T(8,128)(2,1)}, u32[]{:S(2)}, u32[]{:S(2)}) collective-permute-start(bf16[1024,1792]{1,0:T(8,128)(2,1)} %get-tuple-element.18), channel_id=1, source_target_pairs={{0,1},{1,0},{2,3},{3,2},{4,5},{5,4},{6,7},{7,6},{8,9},{9,8},{10,11... | collective-permute-start | bytes 11010056 | tf_op jit(solution)/shard_map/ppermute | solution.py:42
  414.1 10.3 %collective-permute-start.42 = (bf16[2,64,1792]{2,1,0:T(8,128)(2,1)S(1)}, bf16[2,64,1792]{2,1,0:T(8,128)(2,1)S(1)}, u32[]{:S(2)}, u32[]{:S(2)}) collective-permute-start(bf16[2,64,1792]{2,1,0:T(8,128)(2,1)S(1)} %get-tuple-element.42), channel_id=1, source_target_pairs={{0,8},{1,3},{2,10},{3,5},{4,12},{5,7},{6,14},{7,1},{8,16},{9,11},{... | collective-permute-start | bytes 1376264 | tf_op jit(solution)/shard_map/ppermute | solution.py:37
  420.0 14.7 %collective-permute-start.34 = (bf16[4,64,1792]{2,1,0:T(8,128)(2,1)S(1)}, bf16[4,64,1792]{2,1,0:T(8,128)(2,1)S(1)}, u32[]{:S(2)}, u32[]{:S(2)}) collective-permute-start(bf16[4,64,1792]{2,1,0:T(8,128)(2,1)S(1)} %pad_maximum_fusion.4), channel_id=1, source_target_pairs={{0,8},{1,3},{2,10},{3,5},{4,12},{5,7},{6,14},{7,1},{8,16},{9,11},{... | collective-permute-start | bytes 2752520 | tf_op jit(solution)/shard_map/ppermute | solution.py:37
  421.6 13.5 %collective-permute-start.36 = (bf16[4,64,1792]{2,1,0:T(8,128)(2,1)S(1)}, bf16[4,64,1792]{2,1,0:T(8,128)(2,1)S(1)}, u32[]{:S(2)}, u32[]{:S(2)}) collective-permute-start(bf16[4,64,1792]{2,1,0:T(8,128)(2,1)S(1)} %pad_maximum_fusion.5), channel_id=1, source_target_pairs={{0,24},{1,7},{2,26},{3,1},{4,28},{5,3},{6,30},{7,5},{8,0},{9,15},{... | collective-permute-start | bytes 2752520 | tf_op jit(solution)/shard_map/ppermute | solution.py:37
  425.0 20.8 %collective-permute-start.43 = (bf16[4,64,1792]{2,1,0:T(8,128)(2,1)S(1)}, bf16[4,64,1792]{2,1,0:T(8,128)(2,1)S(1)}, u32[]{:S(2)}, u32[]{:S(2)}) collective-permute-start(bf16[4,64,1792]{2,1,0:T(8,128)(2,1)S(1)} %pad_maximum_fusion.6), channel_id=1, source_target_pairs={{0,8},{1,3},{2,10},{3,5},{4,12},{5,7},{6,14},{7,1},{8,16},{9,11},{... | collective-permute-start | bytes 2752520 | tf_op jit(solution)/shard_map/ppermute | solution.py:37
  426.6 19.6 %collective-permute-start.45 = (bf16[4,64,1792]{2,1,0:T(8,128)(2,1)S(1)}, bf16[4,64,1792]{2,1,0:T(8,128)(2,1)S(1)}, u32[]{:S(2)}, u32[]{:S(2)}) collective-permute-start(bf16[4,64,1792]{2,1,0:T(8,128)(2,1)S(1)} %pad_maximum_fusion.7), channel_id=1, source_target_pairs={{0,24},{1,7},{2,26},{3,1},{4,28},{5,3},{6,30},{7,5},{8,0},{9,15},{... | collective-permute-start | bytes 2752520 | tf_op jit(solution)/shard_map/ppermute | solution.py:37
  435.5 14.4 %collective-permute-start.37 = (bf16[32,1792]{1,0:T(8,128)(2,1)S(1)}, bf16[32,1792]{1,0:T(8,128)(2,1)S(1)}, u32[]{:S(2)}, u32[]{:S(2)}) collective-permute-start(bf16[32,1792]{1,0:T(8,128)(2,1)S(1)} %get-tuple-element.52), channel_id=1, source_target_pairs={{0,2},{1,9},{2,4},{3,11},{4,6},{5,13},{6,0},{7,15},{8,10},{9,17},{... | collective-permute-start | bytes 344072 | tf_op jit(solution)/shard_map/ppermute | solution.py:37
  437.1 12.8 %collective-permute-start.39 = (bf16[32,1792]{1,0:T(8,128)(2,1)S(1)}, bf16[32,1792]{1,0:T(8,128)(2,1)S(1)}, u32[]{:S(2)}, u32[]{:S(2)}) collective-permute-start(bf16[32,1792]{1,0:T(8,128)(2,1)S(1)} %get-tuple-element.53), channel_id=1, source_target_pairs={{0,6},{1,25},{2,0},{3,27},{4,2},{5,29},{6,4},{7,31},{8,14},{9,1},{... | collective-permute-start | bytes 344072 | tf_op jit(solution)/shard_map/ppermute | solution.py:37
  (25 other events, 163.6 us)
Sparse Core Ops, SparseCore 0:
  172.3 142.7 all-reduce.3
  317.6 23.5 reduce-scatter.4
  343.7 37.9 reduce-scatter.2
